TPU v7x, 512 devices: a whole 4x8x8 slice. The times are simulated.
512 devices in a mesh: blk: 128 (over x_hi, z, y), chan: 4 (over x_lo, core).
Axes of the slice: x: 4 (x_hi: 2, x_lo: 2; x = x_hi * 2 + x_lo), y: 8, z: 8, core: 2. Of those that a mesh axis runs over, the one named last changes fastest.
Arguments:
- student: bfloat16 [16384, 256], P('blk', 'chan'), may hold values from -11 to 11
- teacher: bfloat16 [16384, 256], P('blk', 'chan'), may hold values from -11 to 11
Outputs:
- student_grad: float32 [16384, 256], P('blk', 'chan')
All inputs are finite; a program needn't handle non-finite values.
Results may differ from a plain program's by a relative error of at most 0.002.
Values may be sent and summed in bfloat16 or wider, within the bound.
No kernel may reach another device: no remote copies, remote signals or barrier semaphores. Data moves between devices by JAX's collectives and lax.ppermute only.
A program may use at most 64 MiB of HBM per device.

v0:
```python
import jax
import jax.numpy as jnp
from jax import lax
from jax.sharding import PartitionSpec as P

inverse_temp = 0.125


def scores(queries, keys, query_index, key_index):
    raw = (
        lax.dot_general(queries, keys, (((1,), (1,)), ((), ())), preferred_element_type=jnp.float32)
        * inverse_temp
    )
    return jnp.where(query_index[:, None] == key_index[None, :], -1e30, raw)


def body(student, teacher):
    n_chan = lax.axis_size("chan")
    chan_index = lax.axis_index("chan")
    blk_index = lax.axis_index("blk")
    row_count = student.shape[0]
    quarter = row_count // n_chan
    slice_width = student.shape[1]
    stud_rows, teach_rows = (
        lax.all_gather(student, "chan", axis=1, tiled=True),
        lax.all_gather(teacher, "chan", axis=1, tiled=True),
    )
    query_index = blk_index * row_count + jnp.arange(row_count, dtype=jnp.int32)
    stud_keys = lax.dynamic_slice_in_dim(stud_rows, chan_index * quarter, quarter, 0)
    teach_keys = lax.dynamic_slice_in_dim(teach_rows, chan_index * quarter, quarter, 0)

    def key_positions(count):
        placed = jnp.arange(count, dtype=jnp.int32)
        return placed // quarter * row_count + chan_index * quarter + placed % quarter

    lowest = jnp.full((row_count,), -1e30, jnp.float32)
    piece = (
        lax.all_gather(stud_keys, "blk", axis=0, tiled=True),
        lax.all_gather(teach_keys, "blk", axis=0, tiled=True),
    )
    key_index = key_positions(piece[0].shape[0])
    stud_score = scores(stud_rows, piece[0], query_index, key_index)
    teach_score = scores(teach_rows, piece[1], query_index, key_index)
    stud_new = jnp.maximum(lowest, jnp.max(stud_score, axis=1))
    teach_new = jnp.maximum(lowest, jnp.max(teach_score, axis=1))
    update_stud_total = jnp.sum(jnp.exp(stud_score - stud_new[:, None]), axis=1)
    update_teach_total = jnp.sum(jnp.exp(teach_score - teach_new[:, None]), axis=1)
    partial_value = (stud_new, update_stud_total, teach_new, update_teach_total)
    stud_max, teach_max = lax.pmax((partial_value[0], partial_value[2]), "chan")
    stud_total, teach_total = lax.psum(
        (
            partial_value[1] * jnp.exp(partial_value[0] - stud_max),
            partial_value[3] * jnp.exp(partial_value[2] - teach_max),
        ),
        "chan",
    )
    piece = (
        lax.all_gather(stud_keys, "blk", axis=0, tiled=True),
        lax.all_gather(teach_keys, "blk", axis=0, tiled=True),
    )
    key_index = key_positions(piece[0].shape[0])
    stud_piece = piece[0]
    stud_score = scores(stud_rows, stud_piece, query_index, key_index)
    teach_score = scores(teach_rows, piece[1], query_index, key_index)
    stud_prob = jnp.exp(stud_score - stud_max[:, None]) / stud_total[:, None]
    teach_prob = jnp.exp(teach_score - teach_max[:, None]) / teach_total[:, None]
    grad_tile = (stud_prob - teach_prob).astype(jnp.bfloat16)
    row_part = jnp.dot(grad_tile, stud_piece, preferred_element_type=jnp.float32)
    col_part = lax.dot_general(
        grad_tile, stud_rows, (((0,), (0,)), ((), ())), preferred_element_type=jnp.float32
    )
    row_part, col_part = (row_part, col_part)
    col_own = lax.psum_scatter(col_part, "blk", scatter_dimension=0, tiled=True)
    summed = lax.psum(row_part, "chan")
    col_rows = lax.all_to_all(col_own, "chan", split_axis=1, concat_axis=0, tiled=True)
    result = lax.dynamic_slice_in_dim(summed, chan_index * slice_width, slice_width, 1) + col_rows
    return inverse_temp * result


def solution(mesh):
    return jax.shard_map(
        body,
        mesh=mesh,
        in_specs=(P("blk", "chan"), P("blk", "chan")),
        out_specs=P("blk", "chan"),
        check_vma=False,
    )
```

profile of v0, /device:TPU:1, one launch (start us, length us, event | category | flops | bytes accessed | tf_op | source)
XLA Modules:
  0.0 1064.9 jit_solution(12224753150180316750)
XLA Ops:
  6.5 12.1 %all_gather.16 = bf16[128,256]{0,1:T(8,128)(2,1)S(1)} all-gather(bf16[128,64]{0,1:T(8,128)(2,1)} %param.3), channel_id=1, replica_groups=mesh['blk'=128,'chan'=4] {'chan'}, dimensions={1}, use_global_device_ids=true | all-gather | bytes 81920 | tf_op jit(solution)/shard_map/all_gather | solution.py:26
  18.7 0.1 constant_dynamic-slice_fusion
  18.8 0.7 copy.11
  19.5 0.0 all-gather.3.cloned.1.call-start
  19.5 5.5 all_gather.14
  25.0 0.1 constant_dynamic-slice_fusion.1
  25.1 0.7 copy.10
  25.8 0.0 reduce-scatter.2.cloned.1.call-start
  25.9 117.1 %all-gather.5.cloned.1.call-done = bf16[4096,256]{1,0:T(8,128)(2,1)} async-done(((bf16[32,256]{1,0:T(8,128)(2,1)}), bf16[4096,256]{1,0:T(8,128)(2,1)}) %all-gather.5.cloned.1.call-update) | async-done | bytes 2097168 | tf_op jit(solution)/shard_map/all_gather | solution.py:59
  143.0 3.5 fusion.14
  146.5 124.4 %all-gather.3.cloned.1.call-done = bf16[4096,256]{1,0:T(8,128)(2,1)} async-done(((bf16[32,256]{1,0:T(8,128)(2,1)}), bf16[4096,256]{1,0:T(8,128)(2,1)}) %all-gather.3.cloned.1.call-update) | async-done | bytes 2097168 | tf_op jit(solution)/shard_map/all_gather | solution.py:58
  270.9 3.2 fusion.15
  274.2 0.6 exponential_reduce_fusion
  274.7 9.7 all-reduce.1
  284.4 2.2 exponential_reduce_fusion.1
  286.6 6.0 all-reduce
  292.6 2.3 subtract_convert_fusion
  294.8 2.6 fusion.17
  297.5 0.0 all-reduce.4.cloned.1.call-start
  297.5 1.5 copy-done
  299.1 1.6 fusion.16
  300.7 614.3 %reduce-scatter.2.cloned.1.call-done = f32[32,256]{1,0:T(8,128)} async-done(((f32[4096,256]{1,0:T(8,128)}), f32[32,256]{1,0:T(8,128)}) %reduce-scatter.2.cloned.1.call-update) | async-done | bytes 32784 | tf_op jit(solution)/shard_map/reduce_scatter | solution.py:73
  915.0 0.8 all_to_all.14
  915.8 0.7 reshape.40
  916.5 106.6 %all-to-all-start = ((f32[4,1,2048]{2,1,0:T(1,128)}), f32[4,1,2048]{2,1,0:T(1,128)S(1)}, u32[]{:S(2)}, u32[]{:S(2)}) async-start(f32[4,1,2048]{2,1,0:T(1,128)} %reshape.40), calls=%async_computation.1 | async-start | bytes 65536 | tf_op jit(solution)/shard_map/all_to_all | solution.py:75
  1023.2 3.3 all-to-all-done
  1026.5 0.5 broadcast.89
  1027.0 0.7 reduce
  1027.7 0.1 reshape.41
  1027.8 0.1 copy.13
  1027.9 29.1 %all-reduce.4.cloned.1.call-done = f32[128,256]{0,1:T(8,128)} async-done(((f32[128,256]{0,1:T(8,128)}), f32[128,256]{0,1:T(8,128)}) %all-reduce.4.cloned.1.call-update) | async-done | bytes 131088 | tf_op jit(solution)/shard_map/psum | solution.py:74
  1057.0 1.4 add_multiply_fusion
  (12 shorter events, 0.1 us)
Async XLA Ops:
  6.5 136.4 %all-gather.5.cloned.1.call-start = ((), (), s32[]{:S(2)}) async-start(), calls=%async_computation.3 | async-start | bytes 2113536 | tf_op jit(solution)/shard_map/all_gather | solution.py:59
  19.5 251.4 %all-gather.3.cloned.1.call-start = ((), (), s32[]{:S(2)}) async-start(), calls=%async_computation.2 | async-start | bytes 2113536 | tf_op jit(solution)/shard_map/all_gather | solution.py:58
  25.8 889.2 %reduce-scatter.2.cloned.1.call-start = ((), (), s32[]{:S(2)}) async-start(), calls=%async_computation.5 | async-start | bytes 4227072 | tf_op jit(solution)/shard_map/reduce_scatter | solution.py:73
  297.5 1.6 copy-start
  297.5 759.5 %all-reduce.4.cloned.1.call-start = ((), (), s32[]{:S(2)}) async-start(), calls=%async_computation.4 | async-start | bytes 262144 | tf_op jit(solution)/shard_map/psum | solution.py:74
  916.5 109.9 %all-to-all-start = ((f32[4,1,2048]{2,1,0:T(1,128)}), f32[4,1,2048]{2,1,0:T(1,128)S(1)}, u32[]{:S(2)}, u32[]{:S(2)}) async-start(f32[4,1,2048]{2,1,0:T(1,128)} %reshape.40), calls=%async_computation.1 | async-start | bytes 65536 | tf_op jit(solution)/shard_map/all_to_all | solution.py:75
Sparse Core Ops, SparseCore 0:
  19.6 123.3 all-gather.4
  147.3 123.5 all-gather.2
  297.6 617.2 reduce-scatter.1
  918.0 138.9 all-reduce.3
where the time goes:
time: 1070 us; the launch traced here: 1060 us
  waiting for transfers between devices  888 us (83%)
  starting transfers between devices  107 us (10%)
  blocking collectives  33.3 us (3%)
  between operations  13.2 us (1%)
  matrix products  11 us (1%)
    reduce_scatter x1, waiting for transfers between devices, body(): col_own = lax.psum_scatter(col_part, 'blk', scatter_dimension=0, tiled=True)  614 us
    all_gather x1, waiting for transfers between devices, body(): lax.all_gather(stud_keys, 'blk', axis=0, tiled=True)  124 us
    all_gather x1, waiting for transfers between devices, body(): lax.all_gather(teach_keys, 'blk', axis=0, tiled=True)  117 us
    all_to_all x1, starting transfers between devices, body(): lax.all_to_all(col_own, 'chan', split_axis=1, concat_axis=0, tiled=True)  107 us
    psum x1, waiting for transfers between devices, body(): summed = lax.psum(row_part, 'chan')  29.1 us
  transfers between devices with their start and end apart: 5, of which 5 were waited for; matrix products, arithmetic and copies ran while one was open for 1% of the time, Pallas kernels for 0%

commit v1 on v0

v1 whole, which is shorter than its diff:
```python
import jax
import jax.numpy as jnp
from jax import lax
from jax.experimental import pallas as pl
from jax.experimental.pallas import tpu as pltpu
from jax.sharding import Mesh, PartitionSpec as P

inverse_temp = 0.125
ROW_BLOCKS = 8
KEYS = 512
QUARTER = 32
CHAN = ("xl", "core")
f32, bf16 = jnp.float32, jnp.bfloat16


def fill_scores(place, rows_ref, keys_ref, score):
    for t in range(2):
        keys = keys_ref[:, t * 256 : (t + 1) * 256]
        for b in range(ROW_BLOCKS):
            rows = jnp.concatenate([rows_ref[b, c, t] for c in range(4)], axis=0)
            score[t, b] = jnp.dot(keys, rows, preferred_element_type=f32) * inverse_temp
    block = place[0]
    first = pl.multiple_of(place[1], QUARTER)
    lane = lax.broadcasted_iota(jnp.int32, (QUARTER, 128), 1) - place[2]
    same = lane == lax.broadcasted_iota(jnp.int32, (QUARTER, 128), 0)
    for t in range(2):
        old = score[t, block, pl.ds(first, QUARTER), :]
        score[t, block, pl.ds(first, QUARTER), :] = jnp.where(same, -1e30, old)


def stats_kernel(place, rows_ref, keys_ref, row_out, col_out, score):
    fill_scores(place, rows_ref, keys_ref, score)
    row_parts, col_parts = [], []
    for t in range(2):
        top = score[t, 0]
        for b in range(1, ROW_BLOCKS):
            top = jnp.maximum(top, score[t, b])
        col_sum = jnp.zeros((KEYS, 128), f32)
        for b in range(ROW_BLOCKS):
            s = score[t, b]
            row_max = jnp.max(s, axis=0, keepdims=True)
            row_sum = jnp.sum(jnp.exp(s - row_max), axis=0, keepdims=True)
            row_parts.append(row_max + jnp.log(row_sum))
            col_sum = col_sum + jnp.exp(s - top)
        top_t, sum_t = top.T, col_sum.T
        col_max = jnp.max(top_t, axis=0, keepdims=True)
        col_tot = jnp.sum(sum_t * jnp.exp(top_t - col_max), axis=0, keepdims=True)
        col = col_max + jnp.log(col_tot)
        col_parts += [col[:, q * 128 : (q + 1) * 128] for q in range(4)]
    row = jnp.concatenate(row_parts, axis=0)
    col = jnp.concatenate(col_parts, axis=0)
    row_out[...] = jnp.broadcast_to(row[None], row_out.shape)
    col_out[...] = jnp.broadcast_to(col[None], col_out.shape)


def combine(parts):
    top = jnp.max(parts, axis=0)
    return top + jnp.log(jnp.sum(jnp.exp(parts - top[None]), axis=0))


def grad_kernel(place, rows_ref, keys_ref, row_in, col_in, out, score):
    fill_scores(place, rows_ref, keys_ref, score)
    row = combine(row_in[...])
    col = combine(col_in[...])

    def key_column(t):
        return jnp.concatenate(
            [jnp.broadcast_to(col[t * 4 + q : t * 4 + q + 1], (128, 128)).T for q in range(4)], axis=0
        )

    cols = [key_column(t) for t in range(2)]
    keys_t = keys_ref[:, 0:256].T
    for b in range(ROW_BLOCKS):
        prob = []
        for t in range(2):
            s = score[t, b]
            prob.append(jnp.exp(s - row[t * 8 + b : t * 8 + b + 1]) + jnp.exp(s - cols[t]))
        tile = prob[0] - prob[1]
        high = tile.astype(bf16)
        low = (tile - high.astype(f32)).astype(bf16)
        part = jnp.dot(keys_t, high, preferred_element_type=f32)
        part = part + jnp.dot(keys_t, low, preferred_element_type=f32)
        out[b] = part.astype(bf16)


VMEM = pl.BlockSpec(memory_space=pltpu.VMEM)
SMEM = pl.BlockSpec(memory_space=pltpu.SMEM)
SCORE = pltpu.VMEM((2, ROW_BLOCKS, KEYS, 128), f32)
PARAMS = pltpu.CompilerParams(vmem_limit_bytes=40 * 1024 * 1024)


def body(student, teacher):
    xh, z, y = lax.axis_index("xh"), lax.axis_index("z"), lax.axis_index("y")
    chan = lax.axis_index(CHAN)
    place = jnp.stack([y, (xh * 8 + z) * QUARTER, chan * QUARTER]).astype(jnp.int32)
    mine = jnp.concatenate([student.T, teacher.T], axis=0)
    own = lax.all_gather(mine, CHAN, axis=0, tiled=True)
    flipped = own.reshape(4, 2, 64, 128).transpose(3, 1, 0, 2).reshape(128, 512)
    share = lax.dynamic_slice_in_dim(flipped, chan * QUARTER, QUARTER, 0)
    keys = lax.all_to_all(
        jnp.broadcast_to(share[None], (16, QUARTER, 512)), ("xh", "z"), split_axis=0, concat_axis=0
    ).reshape(KEYS, 512)
    rows = lax.all_gather(own, "y", axis=0, tiled=True).reshape(8, 4, 2, 64, 128)
    row_part, col_part = pl.pallas_call(
        stats_kernel,
        out_shape=(
            jax.ShapeDtypeStruct((32, 16, 128), f32),
            jax.ShapeDtypeStruct((16, 8, 128), f32),
        ),
        in_specs=[SMEM, VMEM, VMEM],
        out_specs=(VMEM, VMEM),
        scratch_shapes=[SCORE],
        compiler_params=PARAMS,
    )(place, rows, keys)
    row_all = lax.all_to_all(row_part, ("y", "xl", "core"), split_axis=0, concat_axis=0)
    col_all = lax.all_to_all(col_part, ("xh", "z"), split_axis=0, concat_axis=0)
    part = pl.pallas_call(
        grad_kernel,
        out_shape=jax.ShapeDtypeStruct((ROW_BLOCKS, 256, 128), bf16),
        in_specs=[SMEM, VMEM, VMEM, VMEM, VMEM],
        out_specs=VMEM,
        scratch_shapes=[SCORE],
        compiler_params=PARAMS,
    )(place, rows, keys, row_all, col_all)
    got = lax.all_to_all(
        part.reshape(32, 64, 128), ("y", "xl", "core"), split_axis=0, concat_axis=0
    )
    return (inverse_temp * jnp.sum(got.astype(f32), axis=0)).T


def solution(mesh):
    split = Mesh(mesh.devices.reshape(2, 8, 8, 2, 2), ("xh", "z", "y", "xl", "core"))
    spec = P(("xh", "z", "y"), CHAN)
    return jax.shard_map(
        body, mesh=split, in_specs=(spec, spec), out_specs=spec, check_vma=False
    )
```

time: 1070 us -> 133 us (0.12)
  waiting for transfers between devices: 888 us -> 26.6 us
  starting transfers between devices: 107 us -> 7.23 us
  blocking collectives: 33.3 us -> 73.5 us
  matrix products: 11 us -> 0 us
    reduce_scatter x1 -> x0, waiting for transfers between devices: 614 us -> none  [body(): col_own = lax.psum_scatter(col_part, 'blk', scatter_dimension=0, tiled=True)]
    all_gather x2 -> x1, waiting for transfers between devices: 242 us -> 11.4 us  [body(): lax.all_gather(own, 'y', axis=0, tiled=True).reshape(8, 4, 2, 64, 128)]
    all_to_all x1, starting transfers between devices: 107 us -> 7.23 us  [body(): lax.all_to_all(jnp.broadcast_to(share[None], (16, QUARTER, 512)), ('xh',...]
    all_to_all x0 -> x3, blocking collectives: none -> 60.9 us  [the longest x1 22 us: body(): lax.all_to_all(row_part, ('y', 'xl', 'core'), split_axis=0, concat_axis=0)]
    psum x1 -> x0, waiting for transfers between devices: 29.1 us -> none  [body(): summed = lax.psum(row_part, 'chan')]
    all_to_all x1, waiting for transfers between devices: 3.3 us -> 15.2 us  [body(): lax.all_to_all(jnp.broadcast_to(share[None], (16, QUARTER, 512)), ('xh',...]
    dot_general x4 -> x0, matrix products: 11 us -> none  [the longest x2 6.76 us: scores(): lax.dot_general(queries, keys, (((1,), (1,)), ((), ())), preferred_elemen...]
  transfers between devices with their start and end apart: 5 -> 2, of which waited for: 5 -> 2; matrix products, arithmetic and copies ran while one was open for 1% -> 1% of each run, Pallas kernels for 0% -> 0%
where the time goes in v1:
time: 133 us
  blocking collectives  73.5 us (55%)
  waiting for transfers between devices  26.6 us (20%)
  between operations  13.5 us (10%)
  Pallas kernels  7.44 us (6%)
  starting transfers between devices  7.23 us (5%)
  local copies, waits for them, and re-layouts  3.15 us (2%)
  other arithmetic  1.52 us (1%)
    all_to_all x1, blocking collectives, body(): lax.all_to_all(row_part, ('y', 'xl', 'core'), split_axis=0, concat_axis=0)  22 us
    all_to_all x1, blocking collectives, body(): lax.all_to_all(part.reshape(32, 64, 128), ('y', 'xl', 'core'), split_axis...  20.6 us
    all_to_all x1, blocking collectives, body(): col_all = lax.all_to_all(col_part, ('xh', 'z'), split_axis=0, concat_axis=0)  18.3 us
    all_to_all x1, waiting for transfers between devices, body(): lax.all_to_all(jnp.broadcast_to(share[None], (16, QUARTER, 512)), ('xh',...  15.2 us
    all_gather x1, blocking collectives, body(): own = lax.all_gather(mine, CHAN, axis=0, tiled=True)  12.6 us
    all_gather x1, waiting for transfers between devices, body(): lax.all_gather(own, 'y', axis=0, tiled=True).reshape(8, 4, 2, 64, 128)  11.4 us
    all_to_all x1, starting transfers between devices, body(): lax.all_to_all(jnp.broadcast_to(share[None], (16, QUARTER, 512)), ('xh',...  7.23 us
    pallas_call x1, Pallas kernels, body(): pl.pallas_call(grad_kernel, out_shape=jax.ShapeDtypeStruct((ROW_BLOCKS, 2...  3.79 us
  transfers between devices with their start and end apart: 2, of which 2 were waited for; matrix products, arithmetic and copies ran while one was open for 1% of the time, Pallas kernels for 0%

profile of v1, /device:TPU:1, one launch (start us, length us, event | category | flops | bytes accessed | tf_op | source)
XLA Modules:
  0.0 132.9 jit_solution(3997656227710310144)
XLA Ops:
  6.5 0.0 all-gather.2.cloned.1.call-start
  6.5 0.7 pad_maximum_fusion
  7.3 12.6 %all_gather.6 = bf16[512,128]{1,0:T(8,128)(2,1)} all-gather(bf16[128,128]{1,0:T(8,128)(2,1)S(1)} %pad_maximum_fusion), channel_id=1, replica_groups=mesh['xh'=2,'z'=8,'y'=8,'xl'=2,'core'=2] {'xl','core'}, dimensions={0}, use_global_device_ids=true | all-gather | bytes 163840 | tf_op jit(solution)/shard_map/all_gather | solution.py:97
  19.8 0.0 copy-start.1
  19.8 0.0 all-gather.2.cloned.1.call-update
  19.9 0.9 copy-done.1
  20.8 0.1 constant_dynamic-slice_fusion
  20.9 0.1 copy.5
  21.0 0.9 broadcast_in_dim.2
  21.8 7.2 %all-to-all-start = ((bf16[16,32,512]{2,1,0:T(8,128)(2,1)}), bf16[16,32,512]{2,1,0:T(8,128)(2,1)S(1)}, u32[]{:S(2)}, u32[]{:S(2)}) async-start(bf16[16,32,512]{2,1,0:T(8,128)(2,1)} %broadcast_in_dim.2), calls=%async_computation | async-start | bytes 1048576 | tf_op jit(solution)/shard_map/all_to_all | solution.py:100
  29.1 0.1 pad_add_fusion.place
  29.2 15.2 %all-to-all-done = bf16[16,32,512]{2,1,0:T(8,128)(2,1)S(1)} async-done(((bf16[16,32,512]{2,1,0:T(8,128)(2,1)}), bf16[16,32,512]{2,1,0:T(8,128)(2,1)S(1)}, u32[]{:S(2)}, u32[]{:S(2)}) %all-to-all-start) | async-done | bytes 524320 | tf_op jit(solution)/shard_map/all_to_all | solution.py:100
  44.3 11.4 %all-gather.2.cloned.1.call-done = bf16[4096,128]{1,0:T(8,128)(2,1)} async-done(((bf16[512,128]{1,0:T(8,128)(2,1)}), bf16[4096,128]{1,0:T(8,128)(2,1)}) %all-gather.2.cloned.1.call-update) | async-done | bytes 1048592 | tf_op jit(solution)/shard_map/all_gather | solution.py:103
  55.7 0.0 copy-start
  55.7 1.2 copy-done
  57.0 3.6 %shard_map.28 = (f32[32,16,128]{2,1,0:T(8,128)S(1)}, f32[16,8,128]{2,1,0:T(8,128)S(1)}) custom-call(s32[3]{0:T(128)S(1)} %pad_add_fusion.place, bf16[8,4,2,64,128]{4,3,2,1,0:T(8,128)(2,1)S(1)} %bitcast.16, bf16[512,512]{1,0:T(8,128)(2,1)S(1)} %bitcast.14), custom_call_target="tpu_custom_call" | custom-call | tf_op jit(solution)/shard_map/pallas_call | solution.py:104
  60.6 18.3 %all_to_all.20.col_in = f32[16,8,128]{2,1,0:T(8,128)S(1)} all-to-all(f32[16,8,128]{2,1,0:T(8,128)S(1)} %get-tuple-element.8), channel_id=1, replica_groups=mesh['xh'=2,'z'=8,'y'=8,'xl'=2,'core'=2] {'xh','z'}, dimensions={0} | all-to-all | bytes 131072 | tf_op jit(solution)/shard_map/all_to_all | solution.py:116
  78.9 22.0 %all_to_all.21.row_in = f32[32,16,128]{2,1,0:T(8,128)S(1)} all-to-all(f32[32,16,128]{2,1,0:T(8,128)S(1)} %get-tuple-element.7), channel_id=1, replica_groups=mesh['xh'=2,'z'=8,'y'=8,'xl'=2,'core'=2] {'y','xl','core'}, dimensions={0} | all-to-all | bytes 524288 | tf_op jit(solution)/shard_map/all_to_all | solution.py:115
  100.9 3.8 %shard_map.29 = bf16[8,256,128]{2,1,0:T(8,128)(2,1)S(1)} custom-call(s32[3]{0:T(128)S(1)} %pad_add_fusion.place, bf16[8,4,2,64,128]{4,3,2,1,0:T(8,128)(2,1)S(1)} %bitcast.17, bf16[512,512]{1,0:T(8,128)(2,1)S(1)} %bitcast.15, f32[32,16,128]{2,1,0:T(8,128)S(1)} %all_to_all.21.row_in, f32[16,8,128]{2,1,0:T(8,128)S(1)} %all_to_all.20.col_in), custom_call_target="tpu_custom_call" | custom-call | tf_op jit(solution)/shard_map/pallas_call | solution.py:117
  104.7 20.6 %all_to_all.22 = bf16[32,64,128]{2,1,0:T(8,128)(2,1)S(1)} all-to-all(bf16[32,64,128]{2,1,0:T(8,128)(2,1)S(1)} %bitcast.18), channel_id=1, replica_groups=mesh['xh'=2,'z'=8,'y'=8,'xl'=2,'core'=2] {'y','xl','core'}, dimensions={0} | all-to-all | bytes 1048576 | tf_op jit(solution)/shard_map/all_to_all | solution.py:125
  125.3 0.1 convert_reduce_fusion
  125.4 0.6 multiply_bitcast_fusion
  (1 shorter events, 0.0 us)
Async XLA Ops:
  6.5 49.2 %all-gather.2.cloned.1.call-start = ((), (), s32[]{:S(2)}) async-start(), calls=%async_computation.4 | async-start | bytes 1179648 | tf_op jit(solution)/shard_map/all_gather | solution.py:103
  19.8 0.9 copy-start.1
  21.8 22.5 %all-to-all-start = ((bf16[16,32,512]{2,1,0:T(8,128)(2,1)}), bf16[16,32,512]{2,1,0:T(8,128)(2,1)S(1)}, u32[]{:S(2)}, u32[]{:S(2)}) async-start(bf16[16,32,512]{2,1,0:T(8,128)(2,1)} %broadcast_in_dim.2), calls=%async_computation | async-start | bytes 1048576 | tf_op jit(solution)/shard_map/all_to_all | solution.py:100
  55.7 1.2 copy-start
Sparse Core Ops, SparseCore 0:
  20.0 35.6 all-gather.1

commit v2 on v1

v2 whole, which is shorter than its diff:
```python
import jax
import jax.numpy as jnp
from jax import lax
from jax.experimental import pallas as pl
from jax.experimental.pallas import tpu as pltpu
from jax.sharding import Mesh, PartitionSpec as P

inverse_temp = 0.125
AXES = ("xh", "z", "y", "xl", "core")
SIZES = (2, 8, 8, 2, 2)
CHAN = ("xl", "core")
HALF = 64
ROWS = 512
KEYS = 1024
WIDE = 256
BLOCKS = KEYS // WIDE
f32, bf16 = jnp.float32, jnp.bfloat16


def device(xh, z, y, xl, core):
    return (((xh * 8 + z) * 8 + y) * 2 + xl) * 2 + core


MIXED = [
    [device(xh, z, y, xl, 0) for y in range(8) for xl in range(2)] for xh in range(2) for z in range(8)
] + [[device(xh, z, y, xl, 1) for xh in range(2) for z in range(8)] for y in range(8) for xl in range(2)]


def mixed_exchange(pieces):
    return lax.all_to_all(pieces, AXES, split_axis=0, concat_axis=0, axis_index_groups=MIXED)


def fill_scores(place, data, score):
    core = place[0]
    for t in range(2):
        cut = slice(t * 256, (t + 1) * 256)
        rows = jnp.concatenate([data[0, 2 * y + core, :, cut] for y in range(8)], axis=0)
        for b in range(BLOCKS):
            keys = jnp.concatenate([data[1, 4 * b + k, :, cut] for k in range(4)], axis=0)
            score[t, b] = (
                lax.dot_general(rows, keys, (((1,), (1,)), ((), ())), preferred_element_type=f32)
                * inverse_temp
            )
    first = pl.multiple_of(place[1], HALF)
    lane = lax.broadcasted_iota(jnp.int32, (HALF, WIDE), 1) - place[3]
    same = lane == lax.broadcasted_iota(jnp.int32, (HALF, WIDE), 0)
    for t in range(2):
        old = score[t, place[2], pl.ds(first, HALF), :]
        score[t, place[2], pl.ds(first, HALF), :] = jnp.where(same, -1e30, old)


def stats_kernel(place, data, out, score):
    fill_scores(place, data, score)
    row_parts, col_parts = [], []
    for t in range(2):
        top = score[t, 0]
        for b in range(1, BLOCKS):
            top = jnp.maximum(top, score[t, b])
        row_sum = jnp.zeros((ROWS, WIDE), f32)
        for b in range(BLOCKS):
            s = score[t, b]
            col_max = jnp.max(s, axis=0, keepdims=True)
            col_sum = jnp.sum(jnp.exp(s - col_max), axis=0, keepdims=True)
            col = col_max + jnp.log(col_sum)
            col_parts += [col[:, :128], col[:, 128:]]
            row_sum = row_sum + jnp.exp(s - top)
        top_t, sum_t = top.T, row_sum.T
        row_max = jnp.max(top_t, axis=0, keepdims=True)
        row_tot = jnp.sum(sum_t * jnp.exp(top_t - row_max), axis=0, keepdims=True)
        row = row_max + jnp.log(row_tot)
        row_parts += [row[:, q * 128 : (q + 1) * 128] for q in range(4)]
    out[...] = jnp.concatenate(row_parts + col_parts, axis=0)


def grad_kernel(place, data, parts, out, score, lse, high, low):
    fill_scores(place, data, score)
    for side in range(2):
        every = parts[side]
        top = jnp.max(every, axis=0)
        lse[side] = top + jnp.log(jnp.sum(jnp.exp(every - top[None]), axis=0))
    mine = lse[0, pl.ds(pl.multiple_of(place[0] * 8, 8), 8), :]
    for q in range(4):
        at = slice(q * 128, (q + 1) * 128)
        row = [jnp.broadcast_to(mine[t * 4 + q : t * 4 + q + 1], (128, 128)).T for t in range(2)]
        for b in range(BLOCKS):
            for h in range(2):
                prob = []
                for t in range(2):
                    s = score[t, b, at, h * 128 : (h + 1) * 128]
                    k = t * 8 + b * 2 + h
                    prob.append(jnp.exp(s - row[t]) + jnp.exp(s - lse[1, k : k + 1, :]))
                tile = prob[0] - prob[1]
                top_half = tile.astype(bf16)
                to = slice((2 * b + h) * 128, (2 * b + h + 1) * 128)
                high[at, to] = top_half
                low[at, to] = (tile - top_half.astype(f32)).astype(bf16)
    keys = jnp.concatenate([data[1, k, :, 0:256] for k in range(16)], axis=0)
    part = jnp.dot(high[...], keys, preferred_element_type=f32)
    part = (part + jnp.dot(low[...], keys, preferred_element_type=f32)).astype(bf16)
    for y in range(8):
        for half in range(2):
            out[2 * y + half] = part[y * HALF : (y + 1) * HALF, half * 128 : (half + 1) * 128]


VMEM = pl.BlockSpec(memory_space=pltpu.VMEM)
SMEM = pl.BlockSpec(memory_space=pltpu.SMEM)
SCORE = pltpu.VMEM((2, BLOCKS, ROWS, WIDE), f32)
PARAMS = pltpu.CompilerParams(vmem_limit_bytes=40 * 1024 * 1024)


def body(student, teacher):
    xh, z, y, xl, core = (lax.axis_index(a) for a in AXES)
    line = xh * 8 + z
    shift = jnp.where(core == xl, line % 4 * HALF, -4096)
    place = jnp.stack([core, y * HALF, line // 4, shift]).astype(jnp.int32)

    mine = jnp.concatenate([student.T, teacher.T], axis=0)
    own = lax.all_gather(mine, CHAN, axis=0, tiled=True)
    flipped = own.reshape(4, 2, 64, 128).transpose(3, 1, 0, 2).reshape(128, 512)
    share = lax.dynamic_slice_in_dim(flipped, xl * HALF, HALF, 0)
    got = mixed_exchange(jnp.broadcast_to(share[None], (16, HALF, 512)))
    data = lax.all_gather(got, "core", axis=0)

    stats = pl.pallas_call(
        stats_kernel,
        out_shape=jax.ShapeDtypeStruct((24, 128), f32),
        in_specs=[SMEM, VMEM],
        out_specs=VMEM,
        scratch_shapes=[SCORE],
        compiler_params=PARAMS,
    )(place, data)
    both = lax.all_gather(stats, "core", axis=0)
    rows = both[:, :8].reshape(16, 128)
    cols = jnp.logaddexp(both[0, 8:], both[1, 8:])
    pieces = jnp.where(core == 0, rows, cols)
    met = mixed_exchange(jnp.broadcast_to(pieces[None], (16, 16, 128)))
    parts = lax.all_gather(met, "core", axis=0)

    part = pl.pallas_call(
        grad_kernel,
        out_shape=jax.ShapeDtypeStruct((16, HALF, 128), bf16),
        in_specs=[SMEM, VMEM, VMEM],
        out_specs=VMEM,
        scratch_shapes=[
            SCORE,
            pltpu.VMEM((2, 16, 128), f32),
            pltpu.VMEM((ROWS, KEYS), bf16),
            pltpu.VMEM((ROWS, KEYS), bf16),
        ],
        compiler_params=PARAMS,
    )(place, data, parts)
    terms = lax.all_to_all(part, ("y", "xl"), split_axis=0, concat_axis=0)
    total = inverse_temp * jnp.sum(terms.astype(f32), axis=0)
    whole = lax.all_gather(total, "core", axis=0, tiled=True)
    return jnp.where(core == 0, whole[:, :64], whole[:, 64:])


def solution(mesh):
    split = Mesh(mesh.devices.reshape(SIZES), AXES)
    spec = P(("xh", "z", "y"), CHAN)
    return jax.shard_map(
        body, mesh=split, in_specs=(spec, spec), out_specs=spec, check_vma=False
    )
```

time: 133 us -> 121 us (0.910)
  waiting for transfers between devices: 26.6 us -> 17.7 us
  starting transfers between devices: 7.23 us -> 0.01 us
  blocking collectives: 73.5 us -> 78.6 us
    all_to_all x1 -> x0, waiting for transfers between devices: 15.2 us -> none  [body(): lax.all_to_all(jnp.broadcast_to(share[None], (16, QUARTER, 512)), ('xh',...]
    all_to_all x1 -> x0, starting transfers between devices: 7.23 us -> none  [body(): lax.all_to_all(jnp.broadcast_to(share[None], (16, QUARTER, 512)), ('xh',...]
    all_gather x0 -> x3, blocking collectives: none -> 6.88 us  [the longest x1 3.08 us: body(): whole = lax.all_gather(total, 'core', axis=0, tiled=True)]
    all_gather x1, waiting for transfers between devices: 11.4 us -> 17.7 us  [body(): data = lax.all_gather(got, 'core', axis=0)]
    all_to_all x3, blocking collectives: 60.9 us -> 59.6 us  [the longest x2 41.9 us: mixed_exchange(): lax.all_to_all(pieces, AXES, split_axis=0, concat_axis=0, axis_index_grou...]
  transfers between devices with their start and end apart: 2 -> 1, of which waited for: 2 -> 1; matrix products, arithmetic and copies ran while one was open for 1% -> 0% of each run, Pallas kernels for 0% -> 0%
where the time goes in v2:
time: 121 us
  blocking collectives  78.6 us (65%)
  waiting for transfers between devices  17.7 us (15%)
  between operations  13.5 us (11%)
  Pallas kernels  7.57 us (6%)
  local copies, waits for them, and re-layouts  2.61 us (2%)
    all_to_all x2, blocking collectives, mixed_exchange(): lax.all_to_all(pieces, AXES, split_axis=0, concat_axis=0, axis_index_grou...  41.9 us
    all_to_all x1, blocking collectives, body(): terms = lax.all_to_all(part, ('y', 'xl'), split_axis=0, concat_axis=0)  17.7 us
    all_gather x1, waiting for transfers between devices, body(): data = lax.all_gather(got, 'core', axis=0)  17.7 us
    all_gather x1, blocking collectives, body(): own = lax.all_gather(mine, CHAN, axis=0, tiled=True)  12.1 us
    pallas_call x1, Pallas kernels, body(): pl.pallas_call(grad_kernel, out_shape=jax.ShapeDtypeStruct((16, HALF, 128...  4.62 us
    all_gather x1, blocking collectives, body(): whole = lax.all_gather(total, 'core', axis=0, tiled=True)  3.08 us
    pallas_call x1, Pallas kernels, body(): pl.pallas_call(stats_kernel, out_shape=jax.ShapeDtypeStruct((24, 128), f3...  2.95 us
  transfers between devices with their start and end apart: 1, of which 1 were waited for; matrix products, arithmetic and copies ran while one was open for 0% of the time, Pallas kernels for 0%

profile of v2, /device:TPU:1, one launch (start us, length us, event | category | flops | bytes accessed | tf_op | source)
XLA Modules:
  0.0 120.9 jit_solution(1378125400021228357)
XLA Ops:
  6.5 0.0 all-gather.5.cloned.1.call-start
  6.5 0.7 pad_maximum_fusion
  7.3 12.1 %all_gather.24 = bf16[512,128]{1,0:T(8,128)(2,1)S(1)} all-gather(bf16[128,128]{1,0:T(8,128)(2,1)S(1)} %pad_maximum_fusion), channel_id=1, replica_groups=mesh['xh'=2,'z'=8,'y'=8,'xl'=2,'core'=2] {'xl','core'}, dimensions={0}, use_global_device_ids=true | all-gather | bytes 163840 | tf_op jit(solution)/shard_map/all_gather | solution.py:118
  19.4 0.1 constant_dynamic-slice_fusion
  19.5 0.1 copy.7
  19.6 0.1 broadcast_in_dim.6
  19.7 24.5 %all_to_all.15 = bf16[16,64,512]{2,1,0:T(8,128)(2,1)} all-to-all(bf16[16,64,512]{2,1,0:T(8,128)(2,1)S(1)} %broadcast_in_dim.6), channel_id=1, replica_groups={{0,2,4,6,8,10,12,14,16,18,20,22,24,26,28,30},{32,34,36,38,40,42,44,46,4..., dimensions={0} | all-to-all | bytes 2097152 | tf_op jit(solution)/shard_map/all_to_all | solution.py:30
  44.2 0.0 all-gather.5.cloned.1.call-update
  44.3 0.1 pad_add_fusion.place
  44.4 17.7 %all-gather.5.cloned.1.call-done = bf16[32,64,512]{2,1,0:T(8,128)(2,1)} async-done(((bf16[16,64,512]{2,1,0:T(8,128)(2,1)}), bf16[32,64,512]{2,1,0:T(8,128)(2,1)}) %all-gather.5.cloned.1.call-update) | async-done | bytes 2097168 | tf_op jit(solution)/shard_map/all_gather | solution.py:122
  62.1 0.0 copy-start
  62.1 1.6 %copy-done = bf16[32,64,512]{2,1,0:T(8,128)(2,1)S(1)} copy-done((bf16[32,64,512]{2,1,0:T(8,128)(2,1)S(1)}, bf16[32,64,512]{2,1,0:T(8,128)(2,1)}, u32[]{:S(2)}) %copy-start) | copy-done | bytes 2097176
  63.7 2.9 %shard_map.28 = f32[24,128]{1,0:T(8,128)S(1)} custom-call(s32[4]{0:T(128)S(1)} %pad_add_fusion.place, bf16[2,16,64,512]{3,2,1,0:T(8,128)(2,1)S(1)} %bitcast.21), custom_call_target="tpu_custom_call" | custom-call | tf_op jit(solution)/shard_map/pallas_call | solution.py:124
  66.6 1.8 %all-gather.1 = f32[48,128]{1,0:T(8,128)S(1)} all-gather(f32[24,128]{1,0:T(8,128)S(1)} %shard_map.28), channel_id=3, replica_groups=mesh['xh'=2,'z'=8,'y'=8,'xl'=2,'core'=2] {'core'}, dimensions={0}, use_global_device_ids=true | all-gather | bytes 36864 | tf_op jit(solution)/shard_map/all_gather | solution.py:132
  68.5 17.4 %all_to_all.16 = f32[16,16,128]{2,1,0:T(8,128)S(1)} all-to-all(f32[16,16,128]{2,1,0:T(8,128)S(1)} %broadcast_in_dim.16), channel_id=1, replica_groups={{0,2,4,6,8,10,12,14,16,18,20,22,24,26,28,30},{32,34,36,38,40,42,44,46,4..., dimensions={0} | all-to-all | bytes 262144 | tf_op jit(solution)/shard_map/all_to_all | solution.py:30
  85.8 2.0 %all-gather.2 = f32[32,16,128]{2,1,0:T(8,128)S(1)} all-gather(f32[16,16,128]{2,1,0:T(8,128)S(1)} %all_to_all.16), channel_id=4, replica_groups=mesh['xh'=2,'z'=8,'y'=8,'xl'=2,'core'=2] {'core'}, dimensions={0}, use_global_device_ids=true | all-gather | bytes 393216 | tf_op jit(solution)/shard_map/all_gather | solution.py:137
  87.8 4.6 %shard_map.29 = bf16[16,64,128]{2,1,0:T(8,128)(2,1)S(1)} custom-call(s32[4]{0:T(128)S(1)} %pad_add_fusion.place, bf16[2,16,64,512]{3,2,1,0:T(8,128)(2,1)S(1)} %bitcast.22, f32[2,16,16,128]{3,2,1,0:T(8,128)S(1)} %bitcast.23), custom_call_target="tpu_custom_call" | custom-call | tf_op jit(solution)/shard_map/pallas_call | solution.py:139
  92.4 17.7 %all_to_all.17 = bf16[16,64,128]{2,1,0:T(8,128)(2,1)S(1)} all-to-all(bf16[16,64,128]{2,1,0:T(8,128)(2,1)S(1)} %shard_map.29), channel_id=1, replica_groups=mesh['xh'=2,'z'=8,'y'=8,'xl'=2,'core'=2] {'y','xl'}, dimensions={0} | all-to-all | bytes 524288 | tf_op jit(solution)/shard_map/all_to_all | solution.py:152
  110.2 3.1 %all_gather.31 = f32[128,128]{1,0:T(8,128)S(1)} all-gather(f32[64,128]{1,0:T(8,128)S(1)} %broadcast_multiply_fusion), channel_id=1, replica_groups=mesh['xh'=2,'z'=8,'y'=8,'xl'=2,'core'=2] {'core'}, dimensions={0}, use_global_device_ids=true | all-gather | bytes 98304 | tf_op jit(solution)/shard_map/all_gather | solution.py:154
  113.3 0.1 slice_select_fusion
  113.4 0.7 copy.8
  (5 shorter events, 0.1 us)
Async XLA Ops:
  6.5 55.5 %all-gather.5.cloned.1.call-start = ((), (), s32[]{:S(2)}) async-start(), calls=%async_computation.3 | async-start | bytes 3145728 | tf_op jit(solution)/shard_map/all_gather | solution.py:122
  62.1 1.6 %copy-start = (bf16[32,64,512]{2,1,0:T(8,128)(2,1)S(1)}, bf16[32,64,512]{2,1,0:T(8,128)(2,1)}, u32[]{:S(2)}) copy-start(bf16[32,64,512]{2,1,0:T(8,128)(2,1)} %all-gather.5.cloned.1.call-done) | copy-start | bytes 6291460
Sparse Core Ops, SparseCore 0:
  44.4 17.6 all-gather.4

commit v3 on v2

--- a/solution.py
+++ b/solution.py
@@ -30,17 +30,38 @@
     return lax.all_to_all(pieces, AXES, split_axis=0, concat_axis=0, axis_index_groups=MIXED)
 
 
-def fill_scores(place, data, score):
-    core = place[0]
+def share_kernel(place, own, out, turned):
+    for t in range(2):
+        turned[:, t * 256 : (t + 1) * 256] = jnp.concatenate(
+            [own[c * 128 + t * 64 : c * 128 + (t + 1) * 64, :] for c in range(4)], axis=0
+        ).T
+    share = turned[pl.ds(pl.multiple_of(place[4], HALF), HALF), :]
+    out[...] = jnp.broadcast_to(share[None], out.shape)
+
+
+def by_core(place, own, other, run):
+    @pl.when(place[0] == 0)
+    def _():
+        run(0, own, other)
+
+    @pl.when(place[0] == 1)
+    def _():
+        run(1, other, own)
+
+
+def fill_scores(place, core, row_data, key_data, score):
     for t in range(2):
         cut = slice(t * 256, (t + 1) * 256)
-        rows = jnp.concatenate([data[0, 2 * y + core, :, cut] for y in range(8)], axis=0)
+        rows = jnp.concatenate([row_data[2 * y + core, :, cut] for y in range(8)], axis=0)
         for b in range(BLOCKS):
-            keys = jnp.concatenate([data[1, 4 * b + k, :, cut] for k in range(4)], axis=0)
+            keys = jnp.concatenate([key_data[4 * b + k, :, cut] for k in range(4)], axis=0)
             score[t, b] = (
                 lax.dot_general(rows, keys, (((1,), (1,)), ((), ())), preferred_element_type=f32)
                 * inverse_temp
             )
+
+
+def mask_self(place, score):
     first = pl.multiple_of(place[1], HALF)
     lane = lax.broadcasted_iota(jnp.int32, (HALF, WIDE), 1) - place[3]
     same = lane == lax.broadcasted_iota(jnp.int32, (HALF, WIDE), 0)
@@ -49,8 +70,9 @@
         score[t, place[2], pl.ds(first, HALF), :] = jnp.where(same, -1e30, old)
 
 
-def stats_kernel(place, data, out, score):
-    fill_scores(place, data, score)
+def stats_kernel(place, own, other, out, score):
+    by_core(place, own, other, lambda core, rows, keys: fill_scores(place, core, rows, keys, score))
+    mask_self(place, score)
     row_parts, col_parts = [], []
     for t in range(2):
         top = score[t, 0]
@@ -72,8 +94,22 @@
     out[...] = jnp.concatenate(row_parts + col_parts, axis=0)
 
 
-def grad_kernel(place, data, parts, out, score, lse, high, low):
-    fill_scores(place, data, score)
+def pieces_kernel(place, both, out):
+    rows = jnp.concatenate([both[0, :8], both[1, :8]], axis=0)
+    one, two = both[0, 8:], both[1, 8:]
+    top = jnp.maximum(one, two)
+    cols = top + jnp.log(jnp.exp(one - top) + jnp.exp(two - top))
+    out[...] = jnp.broadcast_to(jnp.where(place[0] == 0, rows, cols)[None], out.shape)
+
+
+def grad_kernel(place, own, other, parts, out, score, lse, high, low, students):
+    def fill(core, row_data, key_data):
+        fill_scores(place, core, row_data, key_data, score)
+        for k in range(16):
+            students[k * HALF : (k + 1) * HALF, :] = key_data[k, :, 0:256]
+
+    by_core(place, own, other, fill)
+    mask_self(place, score)
     for side in range(2):
         every = parts[side]
         top = jnp.max(every, axis=0)
@@ -94,7 +130,7 @@
                 to = slice((2 * b + h) * 128, (2 * b + h + 1) * 128)
                 high[at, to] = top_half
                 low[at, to] = (tile - top_half.astype(f32)).astype(bf16)
-    keys = jnp.concatenate([data[1, k, :, 0:256] for k in range(16)], axis=0)
+    keys = students[...]
     part = jnp.dot(high[...], keys, preferred_element_type=f32)
     part = (part + jnp.dot(low[...], keys, preferred_element_type=f32)).astype(bf16)
     for y in range(8):
@@ -102,57 +138,58 @@
             out[2 * y + half] = part[y * HALF : (y + 1) * HALF, half * 128 : (half + 1) * 128]
 
 
+def sum_kernel(terms, out):
+    total = terms[0].astype(f32)
+    for k in range(1, 16):
+        total = total + terms[k].astype(f32)
+    out[...] = total * inverse_temp
+
+
+def turn_kernel(place, whole, out, turned):
+    turned[...] = whole[...].T
+    out[...] = turned[pl.ds(pl.multiple_of(place[0] * 64, 64), 64), :]
+
+
 VMEM = pl.BlockSpec(memory_space=pltpu.VMEM)
 SMEM = pl.BlockSpec(memory_space=pltpu.SMEM)
 SCORE = pltpu.VMEM((2, BLOCKS, ROWS, WIDE), f32)
 PARAMS = pltpu.CompilerParams(vmem_limit_bytes=40 * 1024 * 1024)
 
 
+def call(kernel, shape, dtype, *args, scratch=()):
+    return pl.pallas_call(
+        kernel,
+        out_shape=jax.ShapeDtypeStruct(shape, dtype),
+        in_specs=[SMEM if a.ndim == 1 else VMEM for a in args],
+        out_specs=VMEM,
+        scratch_shapes=list(scratch),
+        compiler_params=PARAMS,
+    )(*args)
+
+
 def body(student, teacher):
     xh, z, y, xl, core = (lax.axis_index(a) for a in AXES)
     line = xh * 8 + z
     shift = jnp.where(core == xl, line % 4 * HALF, -4096)
-    place = jnp.stack([core, y * HALF, line // 4, shift]).astype(jnp.int32)
+    place = jnp.stack([core, y * HALF, line // 4, shift, xl * HALF]).astype(jnp.int32)
 
     mine = jnp.concatenate([student.T, teacher.T], axis=0)
     own = lax.all_gather(mine, CHAN, axis=0, tiled=True)
-    flipped = own.reshape(4, 2, 64, 128).transpose(3, 1, 0, 2).reshape(128, 512)
-    share = lax.dynamic_slice_in_dim(flipped, xl * HALF, HALF, 0)
-    got = mixed_exchange(jnp.broadcast_to(share[None], (16, HALF, 512)))
-    data = lax.all_gather(got, "core", axis=0)
-
-    stats = pl.pallas_call(
-        stats_kernel,
-        out_shape=jax.ShapeDtypeStruct((24, 128), f32),
-        in_specs=[SMEM, VMEM],
-        out_specs=VMEM,
-        scratch_shapes=[SCORE],
-        compiler_params=PARAMS,
-    )(place, data)
-    both = lax.all_gather(stats, "core", axis=0)
-    rows = both[:, :8].reshape(16, 128)
-    cols = jnp.logaddexp(both[0, 8:], both[1, 8:])
-    pieces = jnp.where(core == 0, rows, cols)
-    met = mixed_exchange(jnp.broadcast_to(pieces[None], (16, 16, 128)))
-    parts = lax.all_gather(met, "core", axis=0)
-
-    part = pl.pallas_call(
-        grad_kernel,
-        out_shape=jax.ShapeDtypeStruct((16, HALF, 128), bf16),
-        in_specs=[SMEM, VMEM, VMEM],
-        out_specs=VMEM,
-        scratch_shapes=[
-            SCORE,
-            pltpu.VMEM((2, 16, 128), f32),
-            pltpu.VMEM((ROWS, KEYS), bf16),
-            pltpu.VMEM((ROWS, KEYS), bf16),
-        ],
-        compiler_params=PARAMS,
-    )(place, data, parts)
+    share = call(share_kernel, (16, HALF, 512), bf16, place, own, scratch=[pltpu.VMEM((128, 512), bf16)])
+    met = mixed_exchange(share)
+    data = (met, lax.ppermute(met, "core", [(0, 1), (1, 0)]))
+
+    stats = call(stats_kernel, (24, 128), f32, place, *data, scratch=[SCORE])
+    pieces = call(pieces_kernel, (16, 16, 128), f32, place, lax.all_gather(stats, "core", axis=0))
+    parts = lax.all_gather(mixed_exchange(pieces), "core", axis=0)
+
+    wide = pltpu.VMEM((ROWS, KEYS), bf16)
+    scratch = [SCORE, pltpu.VMEM((2, 16, 128), f32), wide, wide, pltpu.VMEM((KEYS, 256), bf16)]
+    part = call(grad_kernel, (16, HALF, 128), bf16, place, *data, parts, scratch=scratch)
     terms = lax.all_to_all(part, ("y", "xl"), split_axis=0, concat_axis=0)
-    total = inverse_temp * jnp.sum(terms.astype(f32), axis=0)
+    total = call(sum_kernel, (HALF, 128), f32, terms)
     whole = lax.all_gather(total, "core", axis=0, tiled=True)
-    return jnp.where(core == 0, whole[:, :64], whole[:, 64:])
+    return call(turn_kernel, (64, 128), f32, place, whole, scratch=[pltpu.VMEM((128, 128), f32)]).T
 
 
 def solution(mesh):

time: 121 us -> 90.5 us (0.75)
  waiting for transfers between devices: 17.7 us -> 2.63 us
  between operations: 13.5 us -> 0.05 us
  blocking collectives: 78.6 us -> 76 us
  starting transfers between devices: 0.01 us -> 1.91 us
  local copies, waits for them, and re-layouts: 2.61 us -> 0.82 us
    all_gather x1 -> x0, waiting for transfers between devices: 17.7 us -> none  [body(): data = lax.all_gather(got, 'core', axis=0)]
    all_to_all x1, blocking collectives: 17.7 us -> 14.9 us  [body(): terms = lax.all_to_all(part, ('y', 'xl'), split_axis=0, concat_axis=0)]
    ppermute x0 -> x1, waiting for transfers between devices: none -> 2.63 us  [body(): data = (met, lax.ppermute(met, 'core', [(0, 1), (1, 0)]))]
    ppermute x0 -> x1, starting transfers between devices: none -> 1.91 us  [body(): data = (met, lax.ppermute(met, 'core', [(0, 1), (1, 0)]))]
    pallas_call x2 -> x6, Pallas kernels: 7.57 us -> 8.71 us  [call(): pl.pallas_call(kernel, out_shape=jax.ShapeDtypeStruct(shape, dtype), in_s...]
where the time goes in v3:
time: 90.5 us; the launch traced here: 90.1 us
  blocking collectives  76 us (84%)
  Pallas kernels  8.71 us (10%)
  waiting for transfers between devices  2.63 us (3%)
  starting transfers between devices  1.91 us (2%)
    all_to_all x2, blocking collectives, mixed_exchange(): lax.all_to_all(pieces, AXES, split_axis=0, concat_axis=0, axis_index_grou...  42.1 us
    all_to_all x1, blocking collectives, body(): terms = lax.all_to_all(part, ('y', 'xl'), split_axis=0, concat_axis=0)  14.9 us
    all_gather x1, blocking collectives, body(): own = lax.all_gather(mine, CHAN, axis=0, tiled=True)  12.1 us
    pallas_call x6, Pallas kernels, call(): pl.pallas_call(kernel, out_shape=jax.ShapeDtypeStruct(shape, dtype), in_s...  8.71 us
    all_gather x1, blocking collectives, body(): whole = lax.all_gather(total, 'core', axis=0, tiled=True)  3.08 us
    ppermute x1, waiting for transfers between devices, body(): data = (met, lax.ppermute(met, 'core', [(0, 1), (1, 0)]))  2.63 us
    all_gather x1, blocking collectives, body(): parts = lax.all_gather(mixed_exchange(pieces), 'core', axis=0)  1.98 us
    ppermute x1, starting transfers between devices, body(): data = (met, lax.ppermute(met, 'core', [(0, 1), (1, 0)]))  1.91 us
  transfers between devices with their start and end apart: 1, of which 1 were waited for; matrix products, arithmetic and copies ran while one was open for 0% of the time, Pallas kernels for 0%

profile of v3, /device:TPU:1, one launch (start us, length us, event | category | flops | bytes accessed | tf_op | source)
XLA Modules:
  0.0 90.1 jit_solution(17041481170475782879)
XLA Ops:
  0.0 0.0 copy-start
  0.0 0.0 copy-start.1
  0.0 0.7 copy-done
  0.7 0.0 copy-done.1
  0.7 12.1 %all_gather.18.own = bf16[512,128]{1,0:T(8,128)(2,1)S(1)} all-gather(bf16[128,128]{1,0:T(8,128)(2,1)S(1)} %pad_maximum_fusion), channel_id=1, replica_groups=mesh['xh'=2,'z'=8,'y'=8,'xl'=2,'core'=2] {'xl','core'}, dimensions={0}, use_global_device_ids=true | all-gather | bytes 163840 | tf_op jit(solution)/shard_map/all_gather | solution.py:177
  12.9 0.1 stack.23.place
  12.9 0.7 shard_map.28
  13.6 24.4 %all_to_all.15.own = bf16[16,64,512]{2,1,0:T(8,128)(2,1)S(1)} all-to-all(bf16[16,64,512]{2,1,0:T(8,128)(2,1)S(1)} %shard_map.28), channel_id=1, replica_groups={{0,2,4,6,8,10,12,14,16,18,20,22,24,26,28,30},{32,34,36,38,40,42,44,46,4..., dimensions={0} | all-to-all | bytes 2097152 | tf_op jit(solution)/shard_map/all_to_all | solution.py:30
  38.1 1.9 %collective-permute-start = (bf16[16,64,512]{2,1,0:T(8,128)(2,1)S(1)}, bf16[16,64,512]{2,1,0:T(8,128)(2,1)S(1)}, u32[]{:S(2)}, u32[]{:S(2)}) collective-permute-start(bf16[16,64,512]{2,1,0:T(8,128)(2,1)S(1)} %all_to_all.15.own), channel_id=1, source_target_pairs={{0,1},{1,0},{2,3},{3,2},{4,5},{5,4},{6,7},{7,6},{8,9},{9,8},{10,11... | collective-permute-start | bytes 3145736 | tf_op jit(solution)/shard_map/ppermute | solution.py:180
  40.0 2.6 %collective-permute-done.other = bf16[16,64,512]{2,1,0:T(8,128)(2,1)S(1)} collective-permute-done((bf16[16,64,512]{2,1,0:T(8,128)(2,1)S(1)}, bf16[16,64,512]{2,1,0:T(8,128)(2,1)S(1)}, u32[]{:S(2)}, u32[]{:S(2)}) %collective-permute-start) | collective-permute-done | bytes 1048608 | tf_op jit(solution)/shard_map/ppermute | solution.py:180
  42.6 3.0 %shard_map.29 = f32[24,128]{1,0:T(8,128)S(1)} custom-call(s32[5]{0:T(128)S(1)} %stack.23.place, bf16[16,64,512]{2,1,0:T(8,128)(2,1)S(1)} %all_to_all.15.own, bf16[16,64,512]{2,1,0:T(8,128)(2,1)S(1)} %collective-permute-done.other), custom_call_target="tpu_custom_call" | custom-call | tf_op jit(solution)/shard_map/pallas_call | solution.py:160
  45.6 1.8 %all-gather = f32[48,128]{1,0:T(8,128)S(1)} all-gather(f32[24,128]{1,0:T(8,128)S(1)} %shard_map.29), channel_id=2, replica_groups=mesh['xh'=2,'z'=8,'y'=8,'xl'=2,'core'=2] {'core'}, dimensions={0}, use_global_device_ids=true | all-gather | bytes 36864 | tf_op jit(solution)/shard_map/all_gather | solution.py:183
  47.4 0.6 shard_map.30
  48.0 17.7 %all_to_all.16 = f32[16,16,128]{2,1,0:T(8,128)S(1)} all-to-all(f32[16,16,128]{2,1,0:T(8,128)S(1)} %shard_map.30), channel_id=1, replica_groups={{0,2,4,6,8,10,12,14,16,18,20,22,24,26,28,30},{32,34,36,38,40,42,44,46,4..., dimensions={0} | all-to-all | bytes 262144 | tf_op jit(solution)/shard_map/all_to_all | solution.py:30
  65.6 2.0 %all-gather.1 = f32[32,16,128]{2,1,0:T(8,128)S(1)} all-gather(f32[16,16,128]{2,1,0:T(8,128)S(1)} %all_to_all.16), channel_id=3, replica_groups=mesh['xh'=2,'z'=8,'y'=8,'xl'=2,'core'=2] {'core'}, dimensions={0}, use_global_device_ids=true | all-gather | bytes 393216 | tf_op jit(solution)/shard_map/all_gather | solution.py:184
  67.6 3.2 %shard_map.31 = bf16[16,64,128]{2,1,0:T(8,128)(2,1)S(1)} custom-call(s32[5]{0:T(128)S(1)} %stack.23.place, bf16[16,64,512]{2,1,0:T(8,128)(2,1)S(1)} %all_to_all.15.own, bf16[16,64,512]{2,1,0:T(8,128)(2,1)S(1)} %collective-permute-done.other, f32[2,16,16,128]{3,2,1,0:T(8,128)S(1)} %bitcast.10), custom_call_target="tpu_custom_call" | custom-call | tf_op jit(solution)/shard_map/pallas_call | solution.py:160
  70.8 14.9 %all_to_all.17.terms = bf16[16,64,128]{2,1,0:T(8,128)(2,1)S(1)} all-to-all(bf16[16,64,128]{2,1,0:T(8,128)(2,1)S(1)} %shard_map.31), channel_id=1, replica_groups=mesh['xh'=2,'z'=8,'y'=8,'xl'=2,'core'=2] {'y','xl'}, dimensions={0} | all-to-all | bytes 524288 | tf_op jit(solution)/shard_map/all_to_all | solution.py:189
  85.7 3.1 %all_gather.23.whole = f32[128,128]{1,0:T(8,128)S(1)} all-gather(f32[64,128]{1,0:T(8,128)S(1)} %shard_map.32), channel_id=1, replica_groups=mesh['xh'=2,'z'=8,'y'=8,'xl'=2,'core'=2] {'core'}, dimensions={0}, use_global_device_ids=true | all-gather | bytes 98304 | tf_op jit(solution)/shard_map/all_gather | solution.py:191
  88.8 1.3 %shard_map.33 = f32[64,128]{1,0:T(8,128)} custom-call(s32[5]{0:T(128)S(1)} %stack.23.place, f32[128,128]{1,0:T(8,128)S(1)} %all_gather.23.whole), custom_call_target="tpu_custom_call" | custom-call | tf_op jit(solution)/shard_map/pallas_call | solution.py:160
  (2 shorter events, 0.0 us)
Async XLA Ops:
  0.0 0.7 copy-start
  0.0 0.7 copy-start.1
  38.1 4.5 %collective-permute-start = (bf16[16,64,512]{2,1,0:T(8,128)(2,1)S(1)}, bf16[16,64,512]{2,1,0:T(8,128)(2,1)S(1)}, u32[]{:S(2)}, u32[]{:S(2)}) collective-permute-start(bf16[16,64,512]{2,1,0:T(8,128)(2,1)S(1)} %all_to_all.15.own), channel_id=1, source_target_pairs={{0,1},{1,0},{2,3},{3,2},{4,5},{5,4},{6,7},{7,6},{8,9},{9,8},{10,11... | collective-permute-start | bytes 3145736 | tf_op jit(solution)/shard_map/ppermute | solution.py:180

commit v4 on v3

--- a/solution.py
+++ b/solution.py
@@ -71,35 +71,29 @@
 
 
 def stats_kernel(place, own, other, out, score):
-    by_core(place, own, other, lambda core, rows, keys: fill_scores(place, core, rows, keys, score))
-    mask_self(place, score)
-    row_parts, col_parts = [], []
-    for t in range(2):
-        top = score[t, 0]
-        for b in range(1, BLOCKS):
-            top = jnp.maximum(top, score[t, b])
-        row_sum = jnp.zeros((ROWS, WIDE), f32)
+    for t in range(2):
+        cut = slice(t * 256, (t + 1) * 256)
+        across = jnp.concatenate([other[k, :, cut] for k in range(16)], axis=0)
+        for b in range(BLOCKS):
+            items = jnp.concatenate([own[4 * b + k, :, cut] for k in range(4)], axis=0)
+            score[t, b] = (
+                lax.dot_general(across, items, (((1,), (1,)), ((), ())), preferred_element_type=f32)
+                * inverse_temp
+            )
+    first = pl.multiple_of(place[5], HALF)
+    lane = lax.broadcasted_iota(jnp.int32, (HALF, WIDE), 1) - place[7]
+    same = lane == lax.broadcasted_iota(jnp.int32, (HALF, WIDE), 0)
+    for t in range(2):
+        old = score[t, place[6], pl.ds(first, HALF), :]
+        score[t, place[6], pl.ds(first, HALF), :] = jnp.where(same, -1e30, old)
+    parts = []
+    for t in range(2):
         for b in range(BLOCKS):
             s = score[t, b]
-            col_max = jnp.max(s, axis=0, keepdims=True)
-            col_sum = jnp.sum(jnp.exp(s - col_max), axis=0, keepdims=True)
-            col = col_max + jnp.log(col_sum)
-            col_parts += [col[:, :128], col[:, 128:]]
-            row_sum = row_sum + jnp.exp(s - top)
-        top_t, sum_t = top.T, row_sum.T
-        row_max = jnp.max(top_t, axis=0, keepdims=True)
-        row_tot = jnp.sum(sum_t * jnp.exp(top_t - row_max), axis=0, keepdims=True)
-        row = row_max + jnp.log(row_tot)
-        row_parts += [row[:, q * 128 : (q + 1) * 128] for q in range(4)]
-    out[...] = jnp.concatenate(row_parts + col_parts, axis=0)
-
-
-def pieces_kernel(place, both, out):
-    rows = jnp.concatenate([both[0, :8], both[1, :8]], axis=0)
-    one, two = both[0, 8:], both[1, 8:]
-    top = jnp.maximum(one, two)
-    cols = top + jnp.log(jnp.exp(one - top) + jnp.exp(two - top))
-    out[...] = jnp.broadcast_to(jnp.where(place[0] == 0, rows, cols)[None], out.shape)
+            top = jnp.max(s, axis=0, keepdims=True)
+            part = top + jnp.log(jnp.sum(jnp.exp(s - top), axis=0, keepdims=True))
+            parts += [part[:, :128], part[:, 128:]]
+    out[...] = jnp.broadcast_to(jnp.concatenate(parts, axis=0)[None], out.shape)
 
 
 def grad_kernel(place, own, other, parts, out, score, lse, high, low, students):
@@ -114,10 +108,16 @@
         every = parts[side]
         top = jnp.max(every, axis=0)
         lse[side] = top + jnp.log(jnp.sum(jnp.exp(every - top[None]), axis=0))
-    mine = lse[0, pl.ds(pl.multiple_of(place[0] * 8, 8), 8), :]
+
+    def half(k):
+        one, two = lse[0, k : k + 1, :], lse[0, k + 1 : k + 2, :]
+        low_half = jnp.concatenate([one[:, :HALF], two[:, :HALF]], axis=1)
+        high_half = jnp.concatenate([one[:, HALF:], two[:, HALF:]], axis=1)
+        return jnp.where(place[0] == 0, low_half, high_half)
+
     for q in range(4):
         at = slice(q * 128, (q + 1) * 128)
-        row = [jnp.broadcast_to(mine[t * 4 + q : t * 4 + q + 1], (128, 128)).T for t in range(2)]
+        row = [jnp.broadcast_to(half(t * 8 + 2 * q), (128, 128)).T for t in range(2)]
         for b in range(BLOCKS):
             for h in range(2):
                 prob = []
@@ -171,7 +171,11 @@
     xh, z, y, xl, core = (lax.axis_index(a) for a in AXES)
     line = xh * 8 + z
     shift = jnp.where(core == xl, line % 4 * HALF, -4096)
-    place = jnp.stack([core, y * HALF, line // 4, shift, xl * HALF]).astype(jnp.int32)
+    block = 2 * y + xl
+    mine_at, other_at = jnp.where(core == 0, block, line), jnp.where(core == 0, line, block)
+    place = jnp.stack(
+        [core, y * HALF, line // 4, shift, xl * HALF, other_at * HALF, mine_at // 4, mine_at % 4 * HALF]
+    ).astype(jnp.int32)
 
     mine = jnp.concatenate([student.T, teacher.T], axis=0)
     own = lax.all_gather(mine, CHAN, axis=0, tiled=True)
@@ -179,8 +183,8 @@
     met = mixed_exchange(share)
     data = (met, lax.ppermute(met, "core", [(0, 1), (1, 0)]))
 
-    stats = call(stats_kernel, (24, 128), f32, place, *data, scratch=[SCORE])
-    pieces = call(pieces_kernel, (16, 16, 128), f32, place, lax.all_gather(stats, "core", axis=0))
+    tile = pltpu.VMEM((2, BLOCKS, KEYS, WIDE), f32)
+    pieces = call(stats_kernel, (16, 16, 128), f32, place, *data, scratch=[tile])
     parts = lax.all_gather(mixed_exchange(pieces), "core", axis=0)
 
     wide = pltpu.VMEM((ROWS, KEYS), bf16)

time: 90.5 us -> 88.5 us (0.978)
  blocking collectives: 76 us -> 74.1 us
    all_gather x1 -> x0, blocking collectives: 1.82 us -> none  [body(): lax.all_gather(stats, 'core', axis=0)]
    pallas_call x6 -> x5, Pallas kernels: 8.71 us -> 8.57 us  [call(): pl.pallas_call(kernel, out_shape=jax.ShapeDtypeStruct(shape, dtype), in_s...]
where the time goes in v4:
time: 88.5 us; the launch traced here: 88.1 us
  blocking collectives  74.1 us (84%)
  Pallas kernels  8.57 us (10%)
  waiting for transfers between devices  2.63 us (3%)
  starting transfers between devices  1.91 us (2%)
    all_to_all x2, blocking collectives, mixed_exchange(): lax.all_to_all(pieces, AXES, split_axis=0, concat_axis=0, axis_index_grou...  42.1 us
    all_to_all x1, blocking collectives, body(): terms = lax.all_to_all(part, ('y', 'xl'), split_axis=0, concat_axis=0)  14.9 us
    all_gather x1, blocking collectives, body(): own = lax.all_gather(mine, CHAN, axis=0, tiled=True)  12.1 us
    pallas_call x5, Pallas kernels, call(): pl.pallas_call(kernel, out_shape=jax.ShapeDtypeStruct(shape, dtype), in_s...  8.57 us
    all_gather x1, blocking collectives, body(): whole = lax.all_gather(total, 'core', axis=0, tiled=True)  3.08 us
    ppermute x1, waiting for transfers between devices, body(): data = (met, lax.ppermute(met, 'core', [(0, 1), (1, 0)]))  2.63 us
    all_gather x1, blocking collectives, body(): parts = lax.all_gather(mixed_exchange(pieces), 'core', axis=0)  1.98 us
    ppermute x1, starting transfers between devices, body(): data = (met, lax.ppermute(met, 'core', [(0, 1), (1, 0)]))  1.91 us
  transfers between devices with their start and end apart: 1, of which 1 were waited for; matrix products, arithmetic and copies ran while one was open for 0% of the time, Pallas kernels for 0%

profile of v4, /device:TPU:1, one launch (start us, length us, event | category | flops | bytes accessed | tf_op | source)
XLA Modules:
  0.0 88.1 jit_solution(9231998204776710147)
XLA Ops:
  0.0 0.0 copy-start
  0.0 0.0 copy-start.1
  0.0 0.7 copy-done
  0.7 0.0 copy-done.1
  0.7 12.1 %all_gather.12.own = bf16[512,128]{1,0:T(8,128)(2,1)S(1)} all-gather(bf16[128,128]{1,0:T(8,128)(2,1)S(1)} %pad_maximum_fusion), channel_id=1, replica_groups=mesh['xh'=2,'z'=8,'y'=8,'xl'=2,'core'=2] {'xl','core'}, dimensions={0}, use_global_device_ids=true | all-gather | bytes 163840 | tf_op jit(solution)/shard_map/all_gather | solution.py:181
  12.9 0.1 stack.35.place
  12.9 0.7 shard_map.28
  13.6 24.4 %all_to_all.15.own = bf16[16,64,512]{2,1,0:T(8,128)(2,1)S(1)} all-to-all(bf16[16,64,512]{2,1,0:T(8,128)(2,1)S(1)} %shard_map.28), channel_id=1, replica_groups={{0,2,4,6,8,10,12,14,16,18,20,22,24,26,28,30},{32,34,36,38,40,42,44,46,4..., dimensions={0} | all-to-all | bytes 2097152 | tf_op jit(solution)/shard_map/all_to_all | solution.py:30
  38.1 1.9 %collective-permute-start = (bf16[16,64,512]{2,1,0:T(8,128)(2,1)S(1)}, bf16[16,64,512]{2,1,0:T(8,128)(2,1)S(1)}, u32[]{:S(2)}, u32[]{:S(2)}) collective-permute-start(bf16[16,64,512]{2,1,0:T(8,128)(2,1)S(1)} %all_to_all.15.own), channel_id=1, source_target_pairs={{0,1},{1,0},{2,3},{3,2},{4,5},{5,4},{6,7},{7,6},{8,9},{9,8},{10,11... | collective-permute-start | bytes 3145736 | tf_op jit(solution)/shard_map/ppermute | solution.py:184
  40.0 2.6 %collective-permute-done.other = bf16[16,64,512]{2,1,0:T(8,128)(2,1)S(1)} collective-permute-done((bf16[16,64,512]{2,1,0:T(8,128)(2,1)S(1)}, bf16[16,64,512]{2,1,0:T(8,128)(2,1)S(1)}, u32[]{:S(2)}, u32[]{:S(2)}) %collective-permute-start) | collective-permute-done | bytes 1048608 | tf_op jit(solution)/shard_map/ppermute | solution.py:184
  42.6 3.3 %shard_map.29 = f32[16,16,128]{2,1,0:T(8,128)S(1)} custom-call(s32[8]{0:T(128)S(1)} %stack.35.place, bf16[16,64,512]{2,1,0:T(8,128)(2,1)S(1)} %all_to_all.15.own, bf16[16,64,512]{2,1,0:T(8,128)(2,1)S(1)} %collective-permute-done.other), custom_call_target="tpu_custom_call" | custom-call | tf_op jit(solution)/shard_map/pallas_call | solution.py:160
  45.9 17.6 %all_to_all.16 = f32[16,16,128]{2,1,0:T(8,128)S(1)} all-to-all(f32[16,16,128]{2,1,0:T(8,128)S(1)} %shard_map.29), channel_id=1, replica_groups={{0,2,4,6,8,10,12,14,16,18,20,22,24,26,28,30},{32,34,36,38,40,42,44,46,4..., dimensions={0} | all-to-all | bytes 262144 | tf_op jit(solution)/shard_map/all_to_all | solution.py:30
  63.6 2.0 %all-gather = f32[32,16,128]{2,1,0:T(8,128)S(1)} all-gather(f32[16,16,128]{2,1,0:T(8,128)S(1)} %all_to_all.16), channel_id=2, replica_groups=mesh['xh'=2,'z'=8,'y'=8,'xl'=2,'core'=2] {'core'}, dimensions={0}, use_global_device_ids=true | all-gather | bytes 393216 | tf_op jit(solution)/shard_map/all_gather | solution.py:188
  65.5 3.3 %shard_map.30 = bf16[16,64,128]{2,1,0:T(8,128)(2,1)S(1)} custom-call(s32[8]{0:T(128)S(1)} %stack.35.place, bf16[16,64,512]{2,1,0:T(8,128)(2,1)S(1)} %all_to_all.15.own, bf16[16,64,512]{2,1,0:T(8,128)(2,1)S(1)} %collective-permute-done.other, f32[2,16,16,128]{3,2,1,0:T(8,128)S(1)} %bitcast.12), custom_call_target="tpu_custom_call" | custom-call | tf_op jit(solution)/shard_map/pallas_call | solution.py:160
  68.8 14.9 %all_to_all.17.terms = bf16[16,64,128]{2,1,0:T(8,128)(2,1)S(1)} all-to-all(bf16[16,64,128]{2,1,0:T(8,128)(2,1)S(1)} %shard_map.30), channel_id=1, replica_groups=mesh['xh'=2,'z'=8,'y'=8,'xl'=2,'core'=2] {'y','xl'}, dimensions={0} | all-to-all | bytes 524288 | tf_op jit(solution)/shard_map/all_to_all | solution.py:193
  83.7 3.1 %all_gather.15.whole = f32[128,128]{1,0:T(8,128)S(1)} all-gather(f32[64,128]{1,0:T(8,128)S(1)} %shard_map.31), channel_id=1, replica_groups=mesh['xh'=2,'z'=8,'y'=8,'xl'=2,'core'=2] {'core'}, dimensions={0}, use_global_device_ids=true | all-gather | bytes 98304 | tf_op jit(solution)/shard_map/all_gather | solution.py:195
  86.8 1.3 %shard_map.32 = f32[64,128]{1,0:T(8,128)} custom-call(s32[8]{0:T(128)S(1)} %stack.35.place, f32[128,128]{1,0:T(8,128)S(1)} %all_gather.15.whole), custom_call_target="tpu_custom_call" | custom-call | tf_op jit(solution)/shard_map/pallas_call | solution.py:160
  (2 shorter events, 0.0 us)
Async XLA Ops:
  0.0 0.7 copy-start
  0.0 0.7 copy-start.1
  38.1 4.5 %collective-permute-start = (bf16[16,64,512]{2,1,0:T(8,128)(2,1)S(1)}, bf16[16,64,512]{2,1,0:T(8,128)(2,1)S(1)}, u32[]{:S(2)}, u32[]{:S(2)}) collective-permute-start(bf16[16,64,512]{2,1,0:T(8,128)(2,1)S(1)} %all_to_all.15.own), channel_id=1, source_target_pairs={{0,1},{1,0},{2,3},{3,2},{4,5},{5,4},{6,7},{7,6},{8,9},{9,8},{10,11... | collective-permute-start | bytes 3145736 | tf_op jit(solution)/shard_map/ppermute | solution.py:184

commit v5 on v4

--- a/solution.py
+++ b/solution.py
@@ -30,7 +30,19 @@
     return lax.all_to_all(pieces, AXES, split_axis=0, concat_axis=0, axis_index_groups=MIXED)
 
 
-def share_kernel(place, own, out, turned):
+def position():
+    xh, z, y, xl, core = (lax.axis_index(a) for a in AXES)
+    line = xh * 8 + z
+    shift = jnp.where(core == xl, line % 4 * HALF, -4096)
+    block = 2 * y + xl
+    mine_at, other_at = jnp.where(core == 0, block, line), jnp.where(core == 0, line, block)
+    return (
+        core, y * HALF, line // 4, shift, xl * HALF, other_at * HALF, mine_at // 4, mine_at % 4 * HALF,
+    )
+
+
+def share_kernel(own, out, turned):
+    place = position()
     for t in range(2):
         turned[:, t * 256 : (t + 1) * 256] = jnp.concatenate(
             [own[c * 128 + t * 64 : c * 128 + (t + 1) * 64, :] for c in range(4)], axis=0
@@ -70,7 +82,8 @@
         score[t, place[2], pl.ds(first, HALF), :] = jnp.where(same, -1e30, old)
 
 
-def stats_kernel(place, own, other, out, score):
+def stats_kernel(own, other, out, score):
+    place = position()
     for t in range(2):
         cut = slice(t * 256, (t + 1) * 256)
         across = jnp.concatenate([other[k, :, cut] for k in range(16)], axis=0)
@@ -96,7 +109,9 @@
     out[...] = jnp.broadcast_to(jnp.concatenate(parts, axis=0)[None], out.shape)
 
 
-def grad_kernel(place, own, other, parts, out, score, lse, high, low, students):
+def grad_kernel(own, other, parts, out, score, lse, high, low, students):
+    place = position()
+
     def fill(core, row_data, key_data):
         fill_scores(place, core, row_data, key_data, score)
         for k in range(16):
@@ -145,7 +160,8 @@
     out[...] = total * inverse_temp
 
 
-def turn_kernel(place, whole, out, turned):
+def turn_kernel(whole, out, turned):
+    place = position()
     turned[...] = whole[...].T
     out[...] = turned[pl.ds(pl.multiple_of(place[0] * 64, 64), 64), :]
 
@@ -168,32 +184,23 @@
 
 
 def body(student, teacher):
-    xh, z, y, xl, core = (lax.axis_index(a) for a in AXES)
-    line = xh * 8 + z
-    shift = jnp.where(core == xl, line % 4 * HALF, -4096)
-    block = 2 * y + xl
-    mine_at, other_at = jnp.where(core == 0, block, line), jnp.where(core == 0, line, block)
-    place = jnp.stack(
-        [core, y * HALF, line // 4, shift, xl * HALF, other_at * HALF, mine_at // 4, mine_at % 4 * HALF]
-    ).astype(jnp.int32)
-
     mine = jnp.concatenate([student.T, teacher.T], axis=0)
     own = lax.all_gather(mine, CHAN, axis=0, tiled=True)
-    share = call(share_kernel, (16, HALF, 512), bf16, place, own, scratch=[pltpu.VMEM((128, 512), bf16)])
+    share = call(share_kernel, (16, HALF, 512), bf16, own, scratch=[pltpu.VMEM((128, 512), bf16)])
     met = mixed_exchange(share)
     data = (met, lax.ppermute(met, "core", [(0, 1), (1, 0)]))
 
     tile = pltpu.VMEM((2, BLOCKS, KEYS, WIDE), f32)
-    pieces = call(stats_kernel, (16, 16, 128), f32, place, *data, scratch=[tile])
+    pieces = call(stats_kernel, (16, 16, 128), f32, *data, scratch=[tile])
     parts = lax.all_gather(mixed_exchange(pieces), "core", axis=0)
 
     wide = pltpu.VMEM((ROWS, KEYS), bf16)
     scratch = [SCORE, pltpu.VMEM((2, 16, 128), f32), wide, wide, pltpu.VMEM((KEYS, 256), bf16)]
-    part = call(grad_kernel, (16, HALF, 128), bf16, place, *data, parts, scratch=scratch)
+    part = call(grad_kernel, (16, HALF, 128), bf16, *data, parts, scratch=scratch)
     terms = lax.all_to_all(part, ("y", "xl"), split_axis=0, concat_axis=0)
     total = call(sum_kernel, (HALF, 128), f32, terms)
     whole = lax.all_gather(total, "core", axis=0, tiled=True)
-    return call(turn_kernel, (64, 128), f32, place, whole, scratch=[pltpu.VMEM((128, 128), f32)]).T
+    return call(turn_kernel, (64, 128), f32, whole, scratch=[pltpu.VMEM((128, 128), f32)]).T
 
 
 def solution(mesh):

time: 88.5 us -> 86.3 us (0.975)
  Pallas kernels: 8.57 us -> 6.4 us
    pallas_call x5, Pallas kernels: 8.57 us -> 6.4 us  [call(): pl.pallas_call(kernel, out_shape=jax.ShapeDtypeStruct(shape, dtype), in_s...]
where the time goes in v5:
time: 86.3 us; the launch traced here: 85.8 us
  blocking collectives  74.1 us (86%)
  Pallas kernels  6.4 us (7%)
  waiting for transfers between devices  2.63 us (3%)
  starting transfers between devices  1.91 us (2%)
    all_to_all x2, blocking collectives, mixed_exchange(): lax.all_to_all(pieces, AXES, split_axis=0, concat_axis=0, axis_index_grou...  42.1 us
    all_to_all x1, blocking collectives, body(): terms = lax.all_to_all(part, ('y', 'xl'), split_axis=0, concat_axis=0)  14.9 us
    all_gather x1, blocking collectives, body(): own = lax.all_gather(mine, CHAN, axis=0, tiled=True)  12.1 us
    pallas_call x5, Pallas kernels, call(): pl.pallas_call(kernel, out_shape=jax.ShapeDtypeStruct(shape, dtype), in_s...  6.4 us
    all_gather x1, blocking collectives, body(): whole = lax.all_gather(total, 'core', axis=0, tiled=True)  3.07 us
    ppermute x1, waiting for transfers between devices, body(): data = (met, lax.ppermute(met, 'core', [(0, 1), (1, 0)]))  2.63 us
    all_gather x1, blocking collectives, body(): parts = lax.all_gather(mixed_exchange(pieces), 'core', axis=0)  1.98 us
    ppermute x1, starting transfers between devices, body(): data = (met, lax.ppermute(met, 'core', [(0, 1), (1, 0)]))  1.91 us
  transfers between devices with their start and end apart: 1, of which 1 were waited for; matrix products, arithmetic and copies ran while one was open for 0% of the time, Pallas kernels for 0%

profile of v5, /device:TPU:1, one launch (start us, length us, event | category | flops | bytes accessed | tf_op | source)
XLA Modules:
  0.0 85.8 jit_solution(8973480412929194934)
XLA Ops:
  0.0 0.7 pad_maximum_fusion
  0.7 12.1 %all_gather.12.own = bf16[512,128]{1,0:T(8,128)(2,1)S(1)} all-gather(bf16[128,128]{1,0:T(8,128)(2,1)S(1)} %pad_maximum_fusion), channel_id=1, replica_groups=mesh['xh'=2,'z'=8,'y'=8,'xl'=2,'core'=2] {'xl','core'}, dimensions={0}, use_global_device_ids=true | all-gather | bytes 163840 | tf_op jit(solution)/shard_map/all_gather | solution.py:188
  12.9 0.1 shard_map.28
  13.0 24.4 %all_to_all.15.own = bf16[16,64,512]{2,1,0:T(8,128)(2,1)S(1)} all-to-all(bf16[16,64,512]{2,1,0:T(8,128)(2,1)S(1)} %shard_map.28), channel_id=1, replica_groups={{0,2,4,6,8,10,12,14,16,18,20,22,24,26,28,30},{32,34,36,38,40,42,44,46,4..., dimensions={0} | all-to-all | bytes 2097152 | tf_op jit(solution)/shard_map/all_to_all | solution.py:30
  37.4 1.9 %collective-permute-start = (bf16[16,64,512]{2,1,0:T(8,128)(2,1)S(1)}, bf16[16,64,512]{2,1,0:T(8,128)(2,1)S(1)}, u32[]{:S(2)}, u32[]{:S(2)}) collective-permute-start(bf16[16,64,512]{2,1,0:T(8,128)(2,1)S(1)} %all_to_all.15.own), channel_id=1, source_target_pairs={{0,1},{1,0},{2,3},{3,2},{4,5},{5,4},{6,7},{7,6},{8,9},{9,8},{10,11... | collective-permute-start | bytes 3145736 | tf_op jit(solution)/shard_map/ppermute | solution.py:191
  39.3 2.6 %collective-permute-done.other = bf16[16,64,512]{2,1,0:T(8,128)(2,1)S(1)} collective-permute-done((bf16[16,64,512]{2,1,0:T(8,128)(2,1)S(1)}, bf16[16,64,512]{2,1,0:T(8,128)(2,1)S(1)}, u32[]{:S(2)}, u32[]{:S(2)}) %collective-permute-start) | collective-permute-done | bytes 1048608 | tf_op jit(solution)/shard_map/ppermute | solution.py:191
  42.0 2.8 %shard_map.29 = f32[16,16,128]{2,1,0:T(8,128)S(1)} custom-call(bf16[16,64,512]{2,1,0:T(8,128)(2,1)S(1)} %all_to_all.15.own, bf16[16,64,512]{2,1,0:T(8,128)(2,1)S(1)} %collective-permute-done.other), custom_call_target="tpu_custom_call" | custom-call | tf_op jit(solution)/shard_map/pallas_call | solution.py:176
  44.7 17.7 %all_to_all.16 = f32[16,16,128]{2,1,0:T(8,128)S(1)} all-to-all(f32[16,16,128]{2,1,0:T(8,128)S(1)} %shard_map.29), channel_id=1, replica_groups={{0,2,4,6,8,10,12,14,16,18,20,22,24,26,28,30},{32,34,36,38,40,42,44,46,4..., dimensions={0} | all-to-all | bytes 262144 | tf_op jit(solution)/shard_map/all_to_all | solution.py:30
  62.4 2.0 %all-gather = f32[32,16,128]{2,1,0:T(8,128)S(1)} all-gather(f32[16,16,128]{2,1,0:T(8,128)S(1)} %all_to_all.16), channel_id=2, replica_groups=mesh['xh'=2,'z'=8,'y'=8,'xl'=2,'core'=2] {'core'}, dimensions={0}, use_global_device_ids=true | all-gather | bytes 393216 | tf_op jit(solution)/shard_map/all_gather | solution.py:195
  64.4 2.7 %shard_map.30 = bf16[16,64,128]{2,1,0:T(8,128)(2,1)S(1)} custom-call(bf16[16,64,512]{2,1,0:T(8,128)(2,1)S(1)} %all_to_all.15.own, bf16[16,64,512]{2,1,0:T(8,128)(2,1)S(1)} %collective-permute-done.other, f32[2,16,16,128]{3,2,1,0:T(8,128)S(1)} %bitcast.4), custom_call_target="tpu_custom_call" | custom-call | tf_op jit(solution)/shard_map/pallas_call | solution.py:176
  67.1 14.9 %all_to_all.17.terms = bf16[16,64,128]{2,1,0:T(8,128)(2,1)S(1)} all-to-all(bf16[16,64,128]{2,1,0:T(8,128)(2,1)S(1)} %shard_map.30), channel_id=1, replica_groups=mesh['xh'=2,'z'=8,'y'=8,'xl'=2,'core'=2] {'y','xl'}, dimensions={0} | all-to-all | bytes 524288 | tf_op jit(solution)/shard_map/all_to_all | solution.py:200
  82.0 3.1 %all_gather.15.whole = f32[128,128]{1,0:T(8,128)S(1)} all-gather(f32[64,128]{1,0:T(8,128)S(1)} %shard_map.31), channel_id=1, replica_groups=mesh['xh'=2,'z'=8,'y'=8,'xl'=2,'core'=2] {'core'}, dimensions={0}, use_global_device_ids=true | all-gather | bytes 98304 | tf_op jit(solution)/shard_map/all_gather | solution.py:202
  85.1 0.7 shard_map.32
  (1 shorter events, 0.0 us)
Async XLA Ops:
  37.4 4.5 %collective-permute-start = (bf16[16,64,512]{2,1,0:T(8,128)(2,1)S(1)}, bf16[16,64,512]{2,1,0:T(8,128)(2,1)S(1)}, u32[]{:S(2)}, u32[]{:S(2)}) collective-permute-start(bf16[16,64,512]{2,1,0:T(8,128)(2,1)S(1)} %all_to_all.15.own), channel_id=1, source_target_pairs={{0,1},{1,0},{2,3},{3,2},{4,5},{5,4},{6,7},{7,6},{8,9},{9,8},{10,11... | collective-permute-start | bytes 3145736 | tf_op jit(solution)/shard_map/ppermute | solution.py:191

commit v6 on v5

--- a/solution.py
+++ b/solution.py
@@ -67,10 +67,7 @@
         rows = jnp.concatenate([row_data[2 * y + core, :, cut] for y in range(8)], axis=0)
         for b in range(BLOCKS):
             keys = jnp.concatenate([key_data[4 * b + k, :, cut] for k in range(4)], axis=0)
-            score[t, b] = (
-                lax.dot_general(rows, keys, (((1,), (1,)), ((), ())), preferred_element_type=f32)
-                * inverse_temp
-            )
+            score[t, b] = scaled_product(rows, keys)
 
 
 def mask_self(place, score):
@@ -82,30 +79,42 @@
         score[t, place[2], pl.ds(first, HALF), :] = jnp.where(same, -1e30, old)
 
 
-def stats_kernel(own, other, out, score):
+def mask_chunk(chunk, first, shift, wanted):
+    at = pl.ds(pl.multiple_of(first, HALF), HALF)
+    lane = lax.broadcasted_iota(jnp.int32, (HALF, WIDE), 1) - jnp.where(wanted, shift, -4096)
+    same = lane == lax.broadcasted_iota(jnp.int32, (HALF, WIDE), 0)
+    chunk[at, :] = jnp.where(same, -1e30, chunk[at, :])
+
+
+def scaled_product(left, right):
+    scores = lax.dot_general(left, right, (((1,), (1,)), ((), ())), preferred_element_type=f32)
+    return scores * inverse_temp
+
+
+def stats_kernel(own, other, out, *score):
     place = position()
-    for t in range(2):
-        cut = slice(t * 256, (t + 1) * 256)
-        across = jnp.concatenate([other[k, :, cut] for k in range(16)], axis=0)
-        for b in range(BLOCKS):
-            items = jnp.concatenate([own[4 * b + k, :, cut] for k in range(4)], axis=0)
-            score[t, b] = (
-                lax.dot_general(across, items, (((1,), (1,)), ((), ())), preferred_element_type=f32)
-                * inverse_temp
-            )
-    first = pl.multiple_of(place[5], HALF)
-    lane = lax.broadcasted_iota(jnp.int32, (HALF, WIDE), 1) - place[7]
-    same = lane == lax.broadcasted_iota(jnp.int32, (HALF, WIDE), 0)
-    for t in range(2):
-        old = score[t, place[6], pl.ds(first, HALF), :]
-        score[t, place[6], pl.ds(first, HALF), :] = jnp.where(same, -1e30, old)
+    chunks = [(t, b) for t in range(2) for b in range(BLOCKS)]
+    across = [
+        jnp.concatenate([other[k, :, t * 256 : (t + 1) * 256] for k in range(16)], axis=0) for t in range(2)
+    ]
+
+    def fill(n):
+        t, b = chunks[n]
+        items = jnp.concatenate(
+            [own[4 * b + k, :, t * 256 : (t + 1) * 256] for k in range(4)], axis=0
+        )
+        score[n][...] = scaled_product(across[t], items)
+        mask_chunk(score[n], place[5], place[7], place[6] == b)
+
     parts = []
-    for t in range(2):
-        for b in range(BLOCKS):
-            s = score[t, b]
-            top = jnp.max(s, axis=0, keepdims=True)
-            part = top + jnp.log(jnp.sum(jnp.exp(s - top), axis=0, keepdims=True))
-            parts += [part[:, :128], part[:, 128:]]
+    fill(0)
+    for n in range(len(chunks)):
+        if n + 1 < len(chunks):
+            fill(n + 1)
+        s = score[n][...]
+        top = jnp.max(s, axis=0, keepdims=True)
+        part = top + jnp.log(jnp.sum(jnp.exp(s - top), axis=0, keepdims=True))
+        parts += [part[:, :128], part[:, 128:]]
     out[...] = jnp.broadcast_to(jnp.concatenate(parts, axis=0)[None], out.shape)
 
 
@@ -147,27 +156,31 @@
                 low[at, to] = (tile - top_half.astype(f32)).astype(bf16)
     keys = students[...]
     part = jnp.dot(high[...], keys, preferred_element_type=f32)
-    part = (part + jnp.dot(low[...], keys, preferred_element_type=f32)).astype(bf16)
+    part = part + jnp.dot(low[...], keys, preferred_element_type=f32)
     for y in range(8):
         for half in range(2):
-            out[2 * y + half] = part[y * HALF : (y + 1) * HALF, half * 128 : (half + 1) * 128]
+            block = part[y * HALF : (y + 1) * HALF, half * 128 : (half + 1) * 128]
+            one, two = block[:32], block[32:]
+            for c in range(2):
+                at = slice(c * 64, (c + 1) * 64)
+                piece = jnp.concatenate([one[:, at], two[:, at]], axis=1)
+                out[4 * y + 2 * half + c] = piece.astype(bf16)
 
 
 def sum_kernel(terms, out):
-    total = terms[0].astype(f32)
-    for k in range(1, 16):
-        total = total + terms[k].astype(f32)
-    out[...] = total * inverse_temp
-
-
-def turn_kernel(whole, out, turned):
-    place = position()
-    turned[...] = whole[...].T
-    out[...] = turned[pl.ds(pl.multiple_of(place[0] * 64, 64), 64), :]
+    halves = []
+    for k in range(2):
+        total = terms[k].astype(f32)
+        for n in range(1, 16):
+            total = total + terms[2 * n + k].astype(f32)
+        halves.append(total)
+    turned = (jnp.concatenate(halves, axis=0) * inverse_temp).T
+    out[...] = jnp.concatenate(
+        [turned[g * 64 : (g + 1) * 64, k * 32 : (k + 1) * 32] for k in range(2) for g in range(2)], axis=1
+    )
 
 
 VMEM = pl.BlockSpec(memory_space=pltpu.VMEM)
-SMEM = pl.BlockSpec(memory_space=pltpu.SMEM)
 SCORE = pltpu.VMEM((2, BLOCKS, ROWS, WIDE), f32)
 PARAMS = pltpu.CompilerParams(vmem_limit_bytes=40 * 1024 * 1024)
 
@@ -176,7 +189,7 @@
     return pl.pallas_call(
         kernel,
         out_shape=jax.ShapeDtypeStruct(shape, dtype),
-        in_specs=[SMEM if a.ndim == 1 else VMEM for a in args],
+        in_specs=[VMEM] * len(args),
         out_specs=VMEM,
         scratch_shapes=list(scratch),
         compiler_params=PARAMS,
@@ -190,17 +203,15 @@
     met = mixed_exchange(share)
     data = (met, lax.ppermute(met, "core", [(0, 1), (1, 0)]))
 
-    tile = pltpu.VMEM((2, BLOCKS, KEYS, WIDE), f32)
-    pieces = call(stats_kernel, (16, 16, 128), f32, *data, scratch=[tile])
+    tiles = [pltpu.VMEM((KEYS, WIDE), f32)] * (2 * BLOCKS)
+    pieces = call(stats_kernel, (16, 16, 128), f32, *data, scratch=tiles)
     parts = lax.all_gather(mixed_exchange(pieces), "core", axis=0)
 
     wide = pltpu.VMEM((ROWS, KEYS), bf16)
     scratch = [SCORE, pltpu.VMEM((2, 16, 128), f32), wide, wide, pltpu.VMEM((KEYS, 256), bf16)]
-    part = call(grad_kernel, (16, HALF, 128), bf16, *data, parts, scratch=scratch)
-    terms = lax.all_to_all(part, ("y", "xl"), split_axis=0, concat_axis=0)
-    total = call(sum_kernel, (HALF, 128), f32, terms)
-    whole = lax.all_gather(total, "core", axis=0, tiled=True)
-    return call(turn_kernel, (64, 128), f32, whole, scratch=[pltpu.VMEM((128, 128), f32)]).T
+    part = call(grad_kernel, (32, 32, 128), bf16, *data, parts, scratch=scratch)
+    terms = lax.all_to_all(part, ("y", "xl", "core"), split_axis=0, concat_axis=0)
+    return call(sum_kernel, (64, 128), f32, terms).T
 
 
 def solution(mesh):

time: 86.3 us -> 83.7 us (0.970)
  blocking collectives: 74.1 us -> 71.6 us
    all_gather x1 -> x0, blocking collectives: 3.07 us -> none  [body(): whole = lax.all_gather(total, 'core', axis=0, tiled=True)]
    pallas_call x5 -> x4, Pallas kernels: 6.4 us -> 6.37 us  [call(): pl.pallas_call(kernel, out_shape=jax.ShapeDtypeStruct(shape, dtype), in_s...]
where the time goes in v6:
time: 83.7 us; the launch traced here: 83.3 us
  blocking collectives  71.6 us (86%)
  Pallas kernels  6.37 us (8%)
  waiting for transfers between devices  2.63 us (3%)
  starting transfers between devices  1.91 us (2%)
    all_to_all x2, blocking collectives, mixed_exchange(): lax.all_to_all(pieces, AXES, split_axis=0, concat_axis=0, axis_index_grou...  42.1 us
    all_to_all x1, blocking collectives, body(): lax.all_to_all(part, ('y', 'xl', 'core'), split_axis=0, concat_axis=0)  15.5 us
    all_gather x1, blocking collectives, body(): own = lax.all_gather(mine, CHAN, axis=0, tiled=True)  12.1 us
    pallas_call x4, Pallas kernels, call(): pl.pallas_call(kernel, out_shape=jax.ShapeDtypeStruct(shape, dtype), in_s...  6.37 us
    ppermute x1, waiting for transfers between devices, body(): data = (met, lax.ppermute(met, 'core', [(0, 1), (1, 0)]))  2.63 us
    all_gather x1, blocking collectives, body(): parts = lax.all_gather(mixed_exchange(pieces), 'core', axis=0)  1.98 us
    ppermute x1, starting transfers between devices, body(): data = (met, lax.ppermute(met, 'core', [(0, 1), (1, 0)]))  1.91 us
  transfers between devices with their start and end apart: 1, of which 1 were waited for; matrix products, arithmetic and copies ran while one was open for 0% of the time, Pallas kernels for 0%

profile of v6, /device:TPU:1, one launch (start us, length us, event | category | flops | bytes accessed | tf_op | source)
XLA Modules:
  0.0 83.3 jit_solution(11164887280919756282)
XLA Ops:
  0.0 0.7 pad_maximum_fusion
  0.7 12.1 %all_gather.9.own = bf16[512,128]{1,0:T(8,128)(2,1)S(1)} all-gather(bf16[128,128]{1,0:T(8,128)(2,1)S(1)} %pad_maximum_fusion), channel_id=1, replica_groups=mesh['xh'=2,'z'=8,'y'=8,'xl'=2,'core'=2] {'xl','core'}, dimensions={0}, use_global_device_ids=true | all-gather | bytes 163840 | tf_op jit(solution)/shard_map/all_gather | solution.py:201
  12.9 0.1 shard_map.28
  13.0 24.4 %all_to_all.15.own = bf16[16,64,512]{2,1,0:T(8,128)(2,1)S(1)} all-to-all(bf16[16,64,512]{2,1,0:T(8,128)(2,1)S(1)} %shard_map.28), channel_id=1, replica_groups={{0,2,4,6,8,10,12,14,16,18,20,22,24,26,28,30},{32,34,36,38,40,42,44,46,4..., dimensions={0} | all-to-all | bytes 2097152 | tf_op jit(solution)/shard_map/all_to_all | solution.py:30
  37.4 1.9 %collective-permute-start = (bf16[16,64,512]{2,1,0:T(8,128)(2,1)S(1)}, bf16[16,64,512]{2,1,0:T(8,128)(2,1)S(1)}, u32[]{:S(2)}, u32[]{:S(2)}) collective-permute-start(bf16[16,64,512]{2,1,0:T(8,128)(2,1)S(1)} %all_to_all.15.own), channel_id=1, source_target_pairs={{0,1},{1,0},{2,3},{3,2},{4,5},{5,4},{6,7},{7,6},{8,9},{9,8},{10,11... | collective-permute-start | bytes 3145736 | tf_op jit(solution)/shard_map/ppermute | solution.py:204
  39.3 2.6 %collective-permute-done.other = bf16[16,64,512]{2,1,0:T(8,128)(2,1)S(1)} collective-permute-done((bf16[16,64,512]{2,1,0:T(8,128)(2,1)S(1)}, bf16[16,64,512]{2,1,0:T(8,128)(2,1)S(1)}, u32[]{:S(2)}, u32[]{:S(2)}) %collective-permute-start) | collective-permute-done | bytes 1048608 | tf_op jit(solution)/shard_map/ppermute | solution.py:204
  42.0 2.6 %shard_map.29 = f32[16,16,128]{2,1,0:T(8,128)S(1)} custom-call(bf16[16,64,512]{2,1,0:T(8,128)(2,1)S(1)} %all_to_all.15.own, bf16[16,64,512]{2,1,0:T(8,128)(2,1)S(1)} %collective-permute-done.other), custom_call_target="tpu_custom_call" | custom-call | tf_op jit(solution)/shard_map/pallas_call | solution.py:189
  44.6 17.7 %all_to_all.16 = f32[16,16,128]{2,1,0:T(8,128)S(1)} all-to-all(f32[16,16,128]{2,1,0:T(8,128)S(1)} %shard_map.29), channel_id=1, replica_groups={{0,2,4,6,8,10,12,14,16,18,20,22,24,26,28,30},{32,34,36,38,40,42,44,46,4..., dimensions={0} | all-to-all | bytes 262144 | tf_op jit(solution)/shard_map/all_to_all | solution.py:30
  62.3 2.0 %all-gather = f32[32,16,128]{2,1,0:T(8,128)S(1)} all-gather(f32[16,16,128]{2,1,0:T(8,128)S(1)} %all_to_all.16), channel_id=2, replica_groups=mesh['xh'=2,'z'=8,'y'=8,'xl'=2,'core'=2] {'core'}, dimensions={0}, use_global_device_ids=true | all-gather | bytes 393216 | tf_op jit(solution)/shard_map/all_gather | solution.py:208
  64.3 2.8 %shard_map.30 = bf16[32,32,128]{2,1,0:T(8,128)(2,1)S(1)} custom-call(bf16[16,64,512]{2,1,0:T(8,128)(2,1)S(1)} %all_to_all.15.own, bf16[16,64,512]{2,1,0:T(8,128)(2,1)S(1)} %collective-permute-done.other, f32[2,16,16,128]{3,2,1,0:T(8,128)S(1)} %bitcast.4), custom_call_target="tpu_custom_call" | custom-call | tf_op jit(solution)/shard_map/pallas_call | solution.py:189
  67.0 15.5 %all_to_all.17.terms = bf16[32,32,128]{2,1,0:T(8,128)(2,1)S(1)} all-to-all(bf16[32,32,128]{2,1,0:T(8,128)(2,1)S(1)} %shard_map.30), channel_id=1, replica_groups=mesh['xh'=2,'z'=8,'y'=8,'xl'=2,'core'=2] {'y','xl','core'}, dimensions={0} | all-to-all | bytes 524288 | tf_op jit(solution)/shard_map/all_to_all | solution.py:213
  82.5 0.8 shard_map.31
Async XLA Ops:
  37.4 4.5 %collective-permute-start = (bf16[16,64,512]{2,1,0:T(8,128)(2,1)S(1)}, bf16[16,64,512]{2,1,0:T(8,128)(2,1)S(1)}, u32[]{:S(2)}, u32[]{:S(2)}) collective-permute-start(bf16[16,64,512]{2,1,0:T(8,128)(2,1)S(1)} %all_to_all.15.own), channel_id=1, source_target_pairs={{0,1},{1,0},{2,3},{3,2},{4,5},{5,4},{6,7},{7,6},{8,9},{9,8},{10,11... | collective-permute-start | bytes 3145736 | tf_op jit(solution)/shard_map/ppermute | solution.py:204

commit v7 on v6

v7 whole, which is shorter than its diff:
```python
import jax
import jax.numpy as jnp
from jax import lax
from jax.experimental import pallas as pl
from jax.experimental.pallas import tpu as pltpu
from jax.sharding import Mesh, PartitionSpec as P

inverse_temp = 0.125
AXES = ("xh", "z", "y", "xl", "core")
SIZES = (2, 8, 8, 2, 2)
CHAN = ("xl", "core")
HALF = 64
ROWS = 512
KEYS = 1024
WIDE = 256
BLOCKS = KEYS // WIDE
PART = 32
f32, bf16 = jnp.float32, jnp.bfloat16


def device(xh, z, y, xl, core):
    return (((xh * 8 + z) * 8 + y) * 2 + xl) * 2 + core


MIXED = [
    [device(xh, z, y, xl, 0) for y in range(8) for xl in range(2)] for xh in range(2) for z in range(8)
] + [[device(xh, z, y, xl, 1) for xh in range(2) for z in range(8)] for y in range(8) for xl in range(2)]


WIDER = [
    [device(xh, z, y, xl, 0) for y in range(8) for xh in range(2) for xl in range(2)] for z in range(8)
] + [[device(xh, z, y, xl, 1) for z in range(8) for xh in range(2) for xl in range(2)] for y in range(8)]


def mixed_exchange(pieces, groups):
    return lax.all_to_all(pieces, AXES, split_axis=0, concat_axis=0, axis_index_groups=groups)


def position():
    xh, z, y, xl, core = (lax.axis_index(a) for a in AXES)
    first = core == 0
    return core, jnp.where(first, y, z), jnp.where(first, z, y), xh == xl


def share_kernel(mine, out, turned):
    core = lax.axis_index("core")
    for t in range(2):
        turned[:, t * 128 : (t + 1) * 128] = jnp.concatenate(
            [mine[c * 128 + t * 64 : c * 128 + (t + 1) * 64, :] for c in range(2)], axis=0
        ).T
    for k in range(4):
        half = jnp.where(core == 0, k // 2, k % 2)
        share = turned[pl.ds(pl.multiple_of(half * HALF, HALF), HALF), :]
        for n in range(8):
            out[4 * n + k] = share


def block(data, n, t, at=slice(None)):
    cut = slice(t * 128, (t + 1) * 128)
    return jnp.concatenate([data[2 * n, at, cut], data[2 * n + 1, at, cut]], axis=1)


def blocks(data, first, count, t, at=slice(None)):
    return jnp.concatenate([block(data, first + k, t, at) for k in range(count)], axis=0)


def mask_chunk(chunk, first, shift, wanted):
    at = pl.ds(pl.multiple_of(first, HALF), HALF)
    lane = lax.broadcasted_iota(jnp.int32, (HALF, WIDE), 1) - jnp.where(wanted, shift, -4096)
    same = lane == lax.broadcasted_iota(jnp.int32, (HALF, WIDE), 0)
    chunk[at, :] = jnp.where(same, -1e30, chunk[at, :])


def scaled_product(left, right):
    scores = lax.dot_general(left, right, (((1,), (1,)), ((), ())), preferred_element_type=f32)
    return scores * inverse_temp


def stats_kernel(own, other, out, *score):
    core, line, other_line, overlaps = position()
    chunks = [(t, b) for t in range(2) for b in range(BLOCKS)]
    across = [blocks(other, 0, 16, t) for t in range(2)]

    def fill(n):
        t, b = chunks[n]
        score[n][...] = scaled_product(across[t], blocks(own, 4 * b, 4, t))
        for e in range(2):
            mask_chunk(
                score[n],
                (2 * other_line + e) * HALF,
                line % 2 * 128 + e * HALF,
                jnp.logical_and(overlaps, line // 2 == b),
            )

    parts = []
    fill(0)
    for n in range(len(chunks)):
        if n + 1 < len(chunks):
            fill(n + 1)
        s = score[n][...]
        top = jnp.max(s, axis=0, keepdims=True)
        part = top + jnp.log(jnp.sum(jnp.exp(s - top), axis=0, keepdims=True))
        parts += [part[:, :128], part[:, 128:]]
    out[...] = jnp.broadcast_to(jnp.concatenate(parts, axis=0)[None], out.shape)


def grad_kernel(own, other, parts, out, score, lse, high, low, picked_rows, students):
    core, line, other_line, overlaps = position()
    at_core = pl.ds(pl.multiple_of(core * PART, PART), PART)
    @pl.when(core < 2)
    def _():
        for n in range(16):
            to = slice(n * PART, (n + 1) * PART)
            for half in range(2):
                for t in range(2):
                    cut, at = slice(t * 128, (t + 1) * 128), slice(half * 128, (half + 1) * 128)
                    picked_rows[t, to, at] = own[2 * n + half, at_core, cut]
                    students[t, n * HALF : (n + 1) * HALF, at] = other[2 * n + half, :, cut]
        for t in range(2):
            rows = picked_rows[t]
            for b in range(BLOCKS):
                score[t, b] = scaled_product(rows, students[t, b * WIDE : (b + 1) * WIDE, :])

    for side in range(2):
        every = parts[side]
        top = jnp.max(every, axis=0)
        lse[side] = top + jnp.log(jnp.sum(jnp.exp(every - top[None]), axis=0))
    lane = lax.broadcasted_iota(jnp.int32, (PART, WIDE), 1)
    item = lax.broadcasted_iota(jnp.int32, (PART, WIDE), 0)
    for e in range(2):
        shift = jnp.where(overlaps, other_line % 2 * 128 + e * HALF + core * PART, -4096)
        same = lane - shift == item
        at = pl.ds(pl.multiple_of((2 * line + e) * PART, PART), PART)
        for t in range(2):
            old = score[t, other_line // 2, at, :]
            score[t, other_line // 2, at, :] = jnp.where(same, -1e30, old)
    mine, others = lse[core], lse[1 - core]

    def of_part(k):
        picked = []
        for c in range(2):
            starts = [e * HALF + c * PART for e in range(2)]
            picked.append(
                jnp.concatenate(
                    [mine[k + d : k + d + 1, at : at + PART] for d in range(2) for at in starts], axis=1
                )
            )
        return jnp.where(core == 0, picked[0], picked[1])

    for q in range(4):
        at = slice(q * 128, (q + 1) * 128)
        row = [jnp.broadcast_to(of_part(t * 8 + 2 * q), (128, 128)).T for t in range(2)]
        for b in range(BLOCKS):
            for h in range(2):
                prob = []
                for t in range(2):
                    s = score[t, b, at, h * 128 : (h + 1) * 128]
                    k = t * 8 + b * 2 + h
                    prob.append(jnp.exp(s - row[t]) + jnp.exp(s - others[k : k + 1, :]))
                tile = prob[0] - prob[1]
                top_half = tile.astype(bf16)
                to = slice((2 * b + h) * 128, (2 * b + h + 1) * 128)
                high[at, to] = top_half
                low[at, to] = (tile - top_half.astype(f32)).astype(bf16)
    part = jnp.dot(high[...], students[0], preferred_element_type=f32)
    part = (part + jnp.dot(low[...], students[0], preferred_element_type=f32)).astype(bf16)
    for n in range(16):
        for half in range(2):
            out[2 * n + half] = part[n * PART : (n + 1) * PART, half * 128 : (half + 1) * 128]


def sum_kernel(terms, out):
    first = lax.axis_index("core") == 0
    sums = []
    for k in range(4):
        total = terms[k].astype(f32)
        for n in range(1, 8):
            total = total + terms[4 * n + k].astype(f32)
        sums.append(total * inverse_temp)
    out[:PART] = sums[0] + jnp.where(first, sums[1], sums[2])
    out[PART:] = sums[3] + jnp.where(first, sums[2], sums[1])


def turn_kernel(whole, out, turned):
    parts = [whole[k * 64 + half * PART : k * 64 + (half + 1) * PART] for half in range(2) for k in range(2)]
    turned[...] = jnp.concatenate(parts, axis=0).T
    out[...] = turned[pl.ds(pl.multiple_of(lax.axis_index("core") * 64, 64), 64), :]


VMEM = pl.BlockSpec(memory_space=pltpu.VMEM)
PARAMS = pltpu.CompilerParams(vmem_limit_bytes=40 * 1024 * 1024)


def call(kernel, shape, dtype, *args, scratch=()):
    return pl.pallas_call(
        kernel,
        out_shape=jax.ShapeDtypeStruct(shape, dtype),
        in_specs=[VMEM] * len(args),
        out_specs=VMEM,
        scratch_shapes=list(scratch),
        compiler_params=PARAMS,
    )(*args)


def body(student, teacher):
    mine = jnp.concatenate([student.T, teacher.T], axis=0)
    chip = lax.all_gather(mine, "core", axis=0, tiled=True)
    share = call(share_kernel, (32, HALF, 256), bf16, chip, scratch=[pltpu.VMEM((128, 256), bf16)])
    own = mixed_exchange(share, WIDER)
    other = lax.ppermute(own, "core", [(0, 1), (1, 0)])

    tiles = [pltpu.VMEM((KEYS, WIDE), f32)] * (2 * BLOCKS)
    pieces = call(stats_kernel, (16, 16, 128), f32, own, other, scratch=tiles)
    parts = lax.all_gather(mixed_exchange(pieces, MIXED), "core", axis=0)

    wide = pltpu.VMEM((ROWS, KEYS), bf16)
    scratch = [pltpu.VMEM((2, BLOCKS, ROWS, WIDE), f32), pltpu.VMEM((2, 16, 128), f32), wide, wide]
    scratch += [pltpu.VMEM((2, ROWS, 256), bf16), pltpu.VMEM((2, KEYS, 256), bf16)]
    part = call(grad_kernel, (32, PART, 128), bf16, own, other, parts, scratch=scratch)
    terms = mixed_exchange(part, WIDER)
    total = call(sum_kernel, (HALF, 128), f32, terms)
    whole = lax.all_gather(total, "core", axis=0, tiled=True)
    return call(turn_kernel, (64, 128), f32, whole, scratch=[pltpu.VMEM((128, 128), f32)]).T


def solution(mesh):
    split = Mesh(mesh.devices.reshape(SIZES), AXES)
    spec = P(("xh", "z", "y"), CHAN)
    return jax.shard_map(
        body, mesh=split, in_specs=(spec, spec), out_specs=spec, check_vma=False
    )
```

time: 83.7 us -> 82.9 us (level)
  blocking collectives: 71.6 us -> 70.7 us
    all_to_all x2 -> x3, blocking collectives: 42.1 us -> 58.5 us  [mixed_exchange(): lax.all_to_all(pieces, AXES, split_axis=0, concat_axis=0, axis_index_grou...]
    all_to_all x1 -> x0, blocking collectives: 15.5 us -> none  [body(): lax.all_to_all(part, ('y', 'xl', 'core'), split_axis=0, concat_axis=0)]
    all_gather x2 -> x3, blocking collectives: 14.1 us -> 12.3 us  [the longest x1 8.37 us: body(): chip = lax.all_gather(mine, 'core', axis=0, tiled=True)]
    pallas_call x4 -> x5, Pallas kernels: 6.37 us -> 6.42 us  [call(): pl.pallas_call(kernel, out_shape=jax.ShapeDtypeStruct(shape, dtype), in_s...]
where the time goes in v7:
time: 82.9 us; the launch traced here: 82.5 us
  blocking collectives  70.7 us (85%)
  Pallas kernels  6.42 us (8%)
  waiting for transfers between devices  2.63 us (3%)
  starting transfers between devices  1.91 us (2%)
    all_to_all x3, blocking collectives, mixed_exchange(): lax.all_to_all(pieces, AXES, split_axis=0, concat_axis=0, axis_index_grou...  58.5 us
    all_gather x1, blocking collectives, body(): chip = lax.all_gather(mine, 'core', axis=0, tiled=True)  8.37 us
    pallas_call x5, Pallas kernels, call(): pl.pallas_call(kernel, out_shape=jax.ShapeDtypeStruct(shape, dtype), in_s...  6.42 us
    ppermute x1, waiting for transfers between devices, body(): other = lax.ppermute(own, 'core', [(0, 1), (1, 0)])  2.63 us
    all_gather x1, blocking collectives, body(): parts = lax.all_gather(mixed_exchange(pieces, MIXED), 'core', axis=0)  1.98 us
    ppermute x1, starting transfers between devices, body(): other = lax.ppermute(own, 'core', [(0, 1), (1, 0)])  1.91 us
    all_gather x1, blocking collectives, body(): whole = lax.all_gather(total, 'core', axis=0, tiled=True)  1.9 us
  transfers between devices with their start and end apart: 1, of which 1 were waited for; matrix products, arithmetic and copies ran while one was open for 0% of the time, Pallas kernels for 0%

profile of v7, /device:TPU:1, one launch (start us, length us, event | category | flops | bytes accessed | tf_op | source)
XLA Modules:
  0.0 82.5 jit_solution(14790319186030977270)
XLA Ops:
  0.0 0.7 pad_maximum_fusion
  0.7 8.4 %all_gather.12.mine = bf16[256,128]{1,0:T(8,128)(2,1)S(1)} all-gather(bf16[128,128]{1,0:T(8,128)(2,1)S(1)} %pad_maximum_fusion), channel_id=1, replica_groups=mesh['xh'=2,'z'=8,'y'=8,'xl'=2,'core'=2] {'core'}, dimensions={0}, use_global_device_ids=true | all-gather | bytes 98304 | tf_op jit(solution)/shard_map/all_gather | solution.py:207
  9.1 0.1 shard_map.28
  9.3 24.9 %all_to_all.15.own = bf16[32,64,256]{2,1,0:T(8,128)(2,1)S(1)} all-to-all(bf16[32,64,256]{2,1,0:T(8,128)(2,1)S(1)} %shard_map.28), channel_id=1, replica_groups={{0,2,256,258,4,6,260,262,8,10,264,266,12,14,268,270,16,18,272,274,20,22..., dimensions={0} | all-to-all | bytes 2097152 | tf_op jit(solution)/shard_map/all_to_all | solution.py:36
  34.2 1.9 %collective-permute-start = (bf16[32,64,256]{2,1,0:T(8,128)(2,1)S(1)}, bf16[32,64,256]{2,1,0:T(8,128)(2,1)S(1)}, u32[]{:S(2)}, u32[]{:S(2)}) collective-permute-start(bf16[32,64,256]{2,1,0:T(8,128)(2,1)S(1)} %all_to_all.15.own), channel_id=1, source_target_pairs={{0,1},{1,0},{2,3},{3,2},{4,5},{5,4},{6,7},{7,6},{8,9},{9,8},{10,11... | collective-permute-start | bytes 3145736 | tf_op jit(solution)/shard_map/ppermute | solution.py:210
  36.1 2.6 %collective-permute-done.other = bf16[32,64,256]{2,1,0:T(8,128)(2,1)S(1)} collective-permute-done((bf16[32,64,256]{2,1,0:T(8,128)(2,1)S(1)}, bf16[32,64,256]{2,1,0:T(8,128)(2,1)S(1)}, u32[]{:S(2)}, u32[]{:S(2)}) %collective-permute-start) | collective-permute-done | bytes 1048608 | tf_op jit(solution)/shard_map/ppermute | solution.py:210
  38.7 2.7 %shard_map.29 = f32[16,16,128]{2,1,0:T(8,128)S(1)} custom-call(bf16[32,64,256]{2,1,0:T(8,128)(2,1)S(1)} %all_to_all.15.own, bf16[32,64,256]{2,1,0:T(8,128)(2,1)S(1)} %collective-permute-done.other), custom_call_target="tpu_custom_call" | custom-call | tf_op jit(solution)/shard_map/pallas_call | solution.py:195
  41.4 19.3 %all_to_all.16 = f32[16,16,128]{2,1,0:T(8,128)S(1)} all-to-all(f32[16,16,128]{2,1,0:T(8,128)S(1)} %shard_map.29), channel_id=1, replica_groups={{0,2,4,6,8,10,12,14,16,18,20,22,24,26,28,30},{32,34,36,38,40,42,44,46,4..., dimensions={0} | all-to-all | bytes 262144 | tf_op jit(solution)/shard_map/all_to_all | solution.py:36
  60.7 2.0 %all-gather = f32[32,16,128]{2,1,0:T(8,128)S(1)} all-gather(f32[16,16,128]{2,1,0:T(8,128)S(1)} %all_to_all.16), channel_id=2, replica_groups=mesh['xh'=2,'z'=8,'y'=8,'xl'=2,'core'=2] {'core'}, dimensions={0}, use_global_device_ids=true | all-gather | bytes 393216 | tf_op jit(solution)/shard_map/all_gather | solution.py:214
  62.7 2.8 %shard_map.30 = bf16[32,32,128]{2,1,0:T(8,128)(2,1)S(1)} custom-call(bf16[32,64,256]{2,1,0:T(8,128)(2,1)S(1)} %all_to_all.15.own, bf16[32,64,256]{2,1,0:T(8,128)(2,1)S(1)} %collective-permute-done.other, f32[2,16,16,128]{3,2,1,0:T(8,128)S(1)} %bitcast.4), custom_call_target="tpu_custom_call" | custom-call | tf_op jit(solution)/shard_map/pallas_call | solution.py:195
  65.5 14.3 %all_to_all.17.terms = bf16[32,32,128]{2,1,0:T(8,128)(2,1)S(1)} all-to-all(bf16[32,32,128]{2,1,0:T(8,128)(2,1)S(1)} %shard_map.30), channel_id=1, replica_groups={{0,2,256,258,4,6,260,262,8,10,264,266,12,14,268,270,16,18,272,274,20,22..., dimensions={0} | all-to-all | bytes 524288 | tf_op jit(solution)/shard_map/all_to_all | solution.py:36
  79.8 1.9 %all_gather.15.whole = f32[128,128]{1,0:T(8,128)S(1)} all-gather(f32[64,128]{1,0:T(8,128)S(1)} %shard_map.31), channel_id=1, replica_groups=mesh['xh'=2,'z'=8,'y'=8,'xl'=2,'core'=2] {'core'}, dimensions={0}, use_global_device_ids=true | all-gather | bytes 98304 | tf_op jit(solution)/shard_map/all_gather | solution.py:222
  81.8 0.7 shard_map.32
  (1 shorter events, 0.0 us)
Async XLA Ops:
  34.2 4.5 %collective-permute-start = (bf16[32,64,256]{2,1,0:T(8,128)(2,1)S(1)}, bf16[32,64,256]{2,1,0:T(8,128)(2,1)S(1)}, u32[]{:S(2)}, u32[]{:S(2)}) collective-permute-start(bf16[32,64,256]{2,1,0:T(8,128)(2,1)S(1)} %all_to_all.15.own), channel_id=1, source_target_pairs={{0,1},{1,0},{2,3},{3,2},{4,5},{5,4},{6,7},{7,6},{8,9},{9,8},{10,11... | collective-permute-start | bytes 3145736 | tf_op jit(solution)/shard_map/ppermute | solution.py:210

commit v8 on v7

--- a/solution.py
+++ b/solution.py
@@ -163,7 +163,7 @@
                 high[at, to] = top_half
                 low[at, to] = (tile - top_half.astype(f32)).astype(bf16)
     part = jnp.dot(high[...], students[0], preferred_element_type=f32)
-    part = (part + jnp.dot(low[...], students[0], preferred_element_type=f32)).astype(bf16)
+    part = part + jnp.dot(low[...], students[0], preferred_element_type=f32)
     for n in range(16):
         for half in range(2):
             out[2 * n + half] = part[n * PART : (n + 1) * PART, half * 128 : (half + 1) * 128]
@@ -173,9 +173,9 @@
     first = lax.axis_index("core") == 0
     sums = []
     for k in range(4):
-        total = terms[k].astype(f32)
+        total = terms[k]
         for n in range(1, 8):
-            total = total + terms[4 * n + k].astype(f32)
+            total = total + terms[4 * n + k]
         sums.append(total * inverse_temp)
     out[:PART] = sums[0] + jnp.where(first, sums[1], sums[2])
     out[PART:] = sums[3] + jnp.where(first, sums[2], sums[1])
@@ -216,7 +216,7 @@
     wide = pltpu.VMEM((ROWS, KEYS), bf16)
     scratch = [pltpu.VMEM((2, BLOCKS, ROWS, WIDE), f32), pltpu.VMEM((2, 16, 128), f32), wide, wide]
     scratch += [pltpu.VMEM((2, ROWS, 256), bf16), pltpu.VMEM((2, KEYS, 256), bf16)]
-    part = call(grad_kernel, (32, PART, 128), bf16, own, other, parts, scratch=scratch)
+    part = call(grad_kernel, (32, PART, 128), f32, own, other, parts, scratch=scratch)
     terms = mixed_exchange(part, WIDER)
     total = call(sum_kernel, (HALF, 128), f32, terms)
     whole = lax.all_gather(total, "core", axis=0, tiled=True)

time: 82.9 us -> 85.2 us (1.028)
  blocking collectives: 70.7 us -> 73.1 us
    all_to_all x3, blocking collectives: 58.5 us -> 60.8 us  [mixed_exchange(): lax.all_to_all(pieces, AXES, split_axis=0, concat_axis=0, axis_index_grou...]
where the time goes in v8:
time: 85.2 us; the launch traced here: 84.8 us
  blocking collectives  73.1 us (86%)
  Pallas kernels  6.41 us (8%)
  waiting for transfers between devices  2.63 us (3%)
  starting transfers between devices  1.91 us (2%)
    all_to_all x3, blocking collectives, mixed_exchange(): lax.all_to_all(pieces, AXES, split_axis=0, concat_axis=0, axis_index_grou...  60.8 us
    all_gather x1, blocking collectives, body(): chip = lax.all_gather(mine, 'core', axis=0, tiled=True)  8.37 us
    pallas_call x5, Pallas kernels, call(): pl.pallas_call(kernel, out_shape=jax.ShapeDtypeStruct(shape, dtype), in_s...  6.41 us
    ppermute x1, waiting for transfers between devices, body(): other = lax.ppermute(own, 'core', [(0, 1), (1, 0)])  2.63 us
    all_gather x1, blocking collectives, body(): parts = lax.all_gather(mixed_exchange(pieces, MIXED), 'core', axis=0)  1.98 us
    all_gather x1, blocking collectives, body(): whole = lax.all_gather(total, 'core', axis=0, tiled=True)  1.96 us
    ppermute x1, starting transfers between devices, body(): other = lax.ppermute(own, 'core', [(0, 1), (1, 0)])  1.91 us
  transfers between devices with their start and end apart: 1, of which 1 were waited for; matrix products, arithmetic and copies ran while one was open for 0% of the time, Pallas kernels for 0%

profile of v8, /device:TPU:1, one launch (start us, length us, event | category | flops | bytes accessed | tf_op | source)
XLA Modules:
  0.0 84.8 jit_solution(7807457640801135026)
XLA Ops:
  0.0 0.7 pad_maximum_fusion
  0.7 8.4 %all_gather.12.mine = bf16[256,128]{1,0:T(8,128)(2,1)S(1)} all-gather(bf16[128,128]{1,0:T(8,128)(2,1)S(1)} %pad_maximum_fusion), channel_id=1, replica_groups=mesh['xh'=2,'z'=8,'y'=8,'xl'=2,'core'=2] {'core'}, dimensions={0}, use_global_device_ids=true | all-gather | bytes 98304 | tf_op jit(solution)/shard_map/all_gather | solution.py:207
  9.1 0.1 shard_map.28
  9.3 24.9 %all_to_all.15.own = bf16[32,64,256]{2,1,0:T(8,128)(2,1)S(1)} all-to-all(bf16[32,64,256]{2,1,0:T(8,128)(2,1)S(1)} %shard_map.28), channel_id=1, replica_groups={{0,2,256,258,4,6,260,262,8,10,264,266,12,14,268,270,16,18,272,274,20,22..., dimensions={0} | all-to-all | bytes 2097152 | tf_op jit(solution)/shard_map/all_to_all | solution.py:36
  34.2 1.9 %collective-permute-start = (bf16[32,64,256]{2,1,0:T(8,128)(2,1)S(1)}, bf16[32,64,256]{2,1,0:T(8,128)(2,1)S(1)}, u32[]{:S(2)}, u32[]{:S(2)}) collective-permute-start(bf16[32,64,256]{2,1,0:T(8,128)(2,1)S(1)} %all_to_all.15.own), channel_id=1, source_target_pairs={{0,1},{1,0},{2,3},{3,2},{4,5},{5,4},{6,7},{7,6},{8,9},{9,8},{10,11... | collective-permute-start | bytes 3145736 | tf_op jit(solution)/shard_map/ppermute | solution.py:210
  36.1 2.6 %collective-permute-done.other = bf16[32,64,256]{2,1,0:T(8,128)(2,1)S(1)} collective-permute-done((bf16[32,64,256]{2,1,0:T(8,128)(2,1)S(1)}, bf16[32,64,256]{2,1,0:T(8,128)(2,1)S(1)}, u32[]{:S(2)}, u32[]{:S(2)}) %collective-permute-start) | collective-permute-done | bytes 1048608 | tf_op jit(solution)/shard_map/ppermute | solution.py:210
  38.7 2.7 %shard_map.29 = f32[16,16,128]{2,1,0:T(8,128)S(1)} custom-call(bf16[32,64,256]{2,1,0:T(8,128)(2,1)S(1)} %all_to_all.15.own, bf16[32,64,256]{2,1,0:T(8,128)(2,1)S(1)} %collective-permute-done.other), custom_call_target="tpu_custom_call" | custom-call | tf_op jit(solution)/shard_map/pallas_call | solution.py:195
  41.4 19.3 %all_to_all.16 = f32[16,16,128]{2,1,0:T(8,128)S(1)} all-to-all(f32[16,16,128]{2,1,0:T(8,128)S(1)} %shard_map.29), channel_id=1, replica_groups={{0,2,4,6,8,10,12,14,16,18,20,22,24,26,28,30},{32,34,36,38,40,42,44,46,4..., dimensions={0} | all-to-all | bytes 262144 | tf_op jit(solution)/shard_map/all_to_all | solution.py:36
  60.7 2.0 %all-gather = f32[32,16,128]{2,1,0:T(8,128)S(1)} all-gather(f32[16,16,128]{2,1,0:T(8,128)S(1)} %all_to_all.16), channel_id=2, replica_groups=mesh['xh'=2,'z'=8,'y'=8,'xl'=2,'core'=2] {'core'}, dimensions={0}, use_global_device_ids=true | all-gather | bytes 393216 | tf_op jit(solution)/shard_map/all_gather | solution.py:214
  62.7 2.8 %shard_map.30 = f32[32,32,128]{2,1,0:T(8,128)S(1)} custom-call(bf16[32,64,256]{2,1,0:T(8,128)(2,1)S(1)} %all_to_all.15.own, bf16[32,64,256]{2,1,0:T(8,128)(2,1)S(1)} %collective-permute-done.other, f32[2,16,16,128]{3,2,1,0:T(8,128)S(1)} %bitcast.4), custom_call_target="tpu_custom_call" | custom-call | tf_op jit(solution)/shard_map/pallas_call | solution.py:195
  65.5 16.6 %all_to_all.17.terms = f32[32,32,128]{2,1,0:T(8,128)S(1)} all-to-all(f32[32,32,128]{2,1,0:T(8,128)S(1)} %shard_map.30), channel_id=1, replica_groups={{0,2,256,258,4,6,260,262,8,10,264,266,12,14,268,270,16,18,272,274,20,22..., dimensions={0} | all-to-all | bytes 1048576 | tf_op jit(solution)/shard_map/all_to_all | solution.py:36
  82.1 2.0 %all_gather.15.whole = f32[128,128]{1,0:T(8,128)S(1)} all-gather(f32[64,128]{1,0:T(8,128)S(1)} %shard_map.31), channel_id=1, replica_groups=mesh['xh'=2,'z'=8,'y'=8,'xl'=2,'core'=2] {'core'}, dimensions={0}, use_global_device_ids=true | all-gather | bytes 98304 | tf_op jit(solution)/shard_map/all_gather | solution.py:222
  84.1 0.7 shard_map.32
  (1 shorter events, 0.0 us)
Async XLA Ops:
  34.2 4.5 %collective-permute-start = (bf16[32,64,256]{2,1,0:T(8,128)(2,1)S(1)}, bf16[32,64,256]{2,1,0:T(8,128)(2,1)S(1)}, u32[]{:S(2)}, u32[]{:S(2)}) collective-permute-start(bf16[32,64,256]{2,1,0:T(8,128)(2,1)S(1)} %all_to_all.15.own), channel_id=1, source_target_pairs={{0,1},{1,0},{2,3},{3,2},{4,5},{5,4},{6,7},{7,6},{8,9},{9,8},{10,11... | collective-permute-start | bytes 3145736 | tf_op jit(solution)/shard_map/ppermute | solution.py:210

commit v9 on v7

--- a/solution.py
+++ b/solution.py
@@ -152,12 +152,15 @@
         row = [jnp.broadcast_to(of_part(t * 8 + 2 * q), (128, 128)).T for t in range(2)]
         for b in range(BLOCKS):
             for h in range(2):
-                prob = []
+                by_own, by_other = [], []
                 for t in range(2):
                     s = score[t, b, at, h * 128 : (h + 1) * 128]
                     k = t * 8 + b * 2 + h
-                    prob.append(jnp.exp(s - row[t]) + jnp.exp(s - others[k : k + 1, :]))
-                tile = prob[0] - prob[1]
+                    by_own.append(jnp.exp(s - row[t]))
+                    by_other.append(jnp.exp(s - others[k : k + 1, :]))
+                one, two = by_own[0] - by_own[1], by_other[0] - by_other[1]
+                rounded = one.astype(bf16).astype(f32) + two.astype(bf16).astype(f32)
+                tile = 0.5 * (one + two + rounded)
                 top_half = tile.astype(bf16)
                 to = slice((2 * b + h) * 128, (2 * b + h + 1) * 128)
                 high[at, to] = top_half

time: 82.9 us -> 83.4 us (level)
  no operation moved by 1% of the time
where the time goes in v9:
time: 83.4 us; the launch traced here: 83 us
  blocking collectives  70.7 us (85%)
  Pallas kernels  6.94 us (8%)
  waiting for transfers between devices  2.63 us (3%)
  starting transfers between devices  1.91 us (2%)
    all_to_all x3, blocking collectives, mixed_exchange(): lax.all_to_all(pieces, AXES, split_axis=0, concat_axis=0, axis_index_grou...  58.5 us
    all_gather x1, blocking collectives, body(): chip = lax.all_gather(mine, 'core', axis=0, tiled=True)  8.37 us
    pallas_call x5, Pallas kernels, call(): pl.pallas_call(kernel, out_shape=jax.ShapeDtypeStruct(shape, dtype), in_s...  6.94 us
    ppermute x1, waiting for transfers between devices, body(): other = lax.ppermute(own, 'core', [(0, 1), (1, 0)])  2.63 us
    all_gather x1, blocking collectives, body(): parts = lax.all_gather(mixed_exchange(pieces, MIXED), 'core', axis=0)  1.98 us
    ppermute x1, starting transfers between devices, body(): other = lax.ppermute(own, 'core', [(0, 1), (1, 0)])  1.91 us
    all_gather x1, blocking collectives, body(): whole = lax.all_gather(total, 'core', axis=0, tiled=True)  1.9 us
  transfers between devices with their start and end apart: 1, of which 1 were waited for; matrix products, arithmetic and copies ran while one was open for 0% of the time, Pallas kernels for 0%

profile of v9, /device:TPU:1, one launch (start us, length us, event | category | flops | bytes accessed | tf_op | source)
XLA Modules:
  0.0 83.0 jit_solution(3330542313142221914)
XLA Ops:
  0.0 0.7 pad_maximum_fusion
  0.7 8.4 %all_gather.12.mine = bf16[256,128]{1,0:T(8,128)(2,1)S(1)} all-gather(bf16[128,128]{1,0:T(8,128)(2,1)S(1)} %pad_maximum_fusion), channel_id=1, replica_groups=mesh['xh'=2,'z'=8,'y'=8,'xl'=2,'core'=2] {'core'}, dimensions={0}, use_global_device_ids=true | all-gather | bytes 98304 | tf_op jit(solution)/shard_map/all_gather | solution.py:210
  9.1 0.1 shard_map.28
  9.3 24.9 %all_to_all.15.own = bf16[32,64,256]{2,1,0:T(8,128)(2,1)S(1)} all-to-all(bf16[32,64,256]{2,1,0:T(8,128)(2,1)S(1)} %shard_map.28), channel_id=1, replica_groups={{0,2,256,258,4,6,260,262,8,10,264,266,12,14,268,270,16,18,272,274,20,22..., dimensions={0} | all-to-all | bytes 2097152 | tf_op jit(solution)/shard_map/all_to_all | solution.py:36
  34.2 1.9 %collective-permute-start = (bf16[32,64,256]{2,1,0:T(8,128)(2,1)S(1)}, bf16[32,64,256]{2,1,0:T(8,128)(2,1)S(1)}, u32[]{:S(2)}, u32[]{:S(2)}) collective-permute-start(bf16[32,64,256]{2,1,0:T(8,128)(2,1)S(1)} %all_to_all.15.own), channel_id=1, source_target_pairs={{0,1},{1,0},{2,3},{3,2},{4,5},{5,4},{6,7},{7,6},{8,9},{9,8},{10,11... | collective-permute-start | bytes 3145736 | tf_op jit(solution)/shard_map/ppermute | solution.py:213
  36.1 2.6 %collective-permute-done.other = bf16[32,64,256]{2,1,0:T(8,128)(2,1)S(1)} collective-permute-done((bf16[32,64,256]{2,1,0:T(8,128)(2,1)S(1)}, bf16[32,64,256]{2,1,0:T(8,128)(2,1)S(1)}, u32[]{:S(2)}, u32[]{:S(2)}) %collective-permute-start) | collective-permute-done | bytes 1048608 | tf_op jit(solution)/shard_map/ppermute | solution.py:213
  38.7 2.7 %shard_map.29 = f32[16,16,128]{2,1,0:T(8,128)S(1)} custom-call(bf16[32,64,256]{2,1,0:T(8,128)(2,1)S(1)} %all_to_all.15.own, bf16[32,64,256]{2,1,0:T(8,128)(2,1)S(1)} %collective-permute-done.other), custom_call_target="tpu_custom_call" | custom-call | tf_op jit(solution)/shard_map/pallas_call | solution.py:198
  41.4 19.3 %all_to_all.16 = f32[16,16,128]{2,1,0:T(8,128)S(1)} all-to-all(f32[16,16,128]{2,1,0:T(8,128)S(1)} %shard_map.29), channel_id=1, replica_groups={{0,2,4,6,8,10,12,14,16,18,20,22,24,26,28,30},{32,34,36,38,40,42,44,46,4..., dimensions={0} | all-to-all | bytes 262144 | tf_op jit(solution)/shard_map/all_to_all | solution.py:36
  60.7 2.0 %all-gather = f32[32,16,128]{2,1,0:T(8,128)S(1)} all-gather(f32[16,16,128]{2,1,0:T(8,128)S(1)} %all_to_all.16), channel_id=2, replica_groups=mesh['xh'=2,'z'=8,'y'=8,'xl'=2,'core'=2] {'core'}, dimensions={0}, use_global_device_ids=true | all-gather | bytes 393216 | tf_op jit(solution)/shard_map/all_gather | solution.py:217
  62.7 3.3 %shard_map.30 = bf16[32,32,128]{2,1,0:T(8,128)(2,1)S(1)} custom-call(bf16[32,64,256]{2,1,0:T(8,128)(2,1)S(1)} %all_to_all.15.own, bf16[32,64,256]{2,1,0:T(8,128)(2,1)S(1)} %collective-permute-done.other, f32[2,16,16,128]{3,2,1,0:T(8,128)S(1)} %bitcast.4), custom_call_target="tpu_custom_call" | custom-call | tf_op jit(solution)/shard_map/pallas_call | solution.py:198
  66.0 14.3 %all_to_all.17.terms = bf16[32,32,128]{2,1,0:T(8,128)(2,1)S(1)} all-to-all(bf16[32,32,128]{2,1,0:T(8,128)(2,1)S(1)} %shard_map.30), channel_id=1, replica_groups={{0,2,256,258,4,6,260,262,8,10,264,266,12,14,268,270,16,18,272,274,20,22..., dimensions={0} | all-to-all | bytes 524288 | tf_op jit(solution)/shard_map/all_to_all | solution.py:36
  80.4 1.9 %all_gather.15.whole = f32[128,128]{1,0:T(8,128)S(1)} all-gather(f32[64,128]{1,0:T(8,128)S(1)} %shard_map.31), channel_id=1, replica_groups=mesh['xh'=2,'z'=8,'y'=8,'xl'=2,'core'=2] {'core'}, dimensions={0}, use_global_device_ids=true | all-gather | bytes 98304 | tf_op jit(solution)/shard_map/all_gather | solution.py:225
  82.3 0.7 shard_map.32
  (1 shorter events, 0.0 us)
Async XLA Ops:
  34.2 4.5 %collective-permute-start = (bf16[32,64,256]{2,1,0:T(8,128)(2,1)S(1)}, bf16[32,64,256]{2,1,0:T(8,128)(2,1)S(1)}, u32[]{:S(2)}, u32[]{:S(2)}) collective-permute-start(bf16[32,64,256]{2,1,0:T(8,128)(2,1)S(1)} %all_to_all.15.own), channel_id=1, source_target_pairs={{0,1},{1,0},{2,3},{3,2},{4,5},{5,4},{6,7},{7,6},{8,9},{9,8},{10,11... | collective-permute-start | bytes 3145736 | tf_op jit(solution)/shard_map/ppermute | solution.py:213

commit v10 on v9

--- a/solution.py
+++ b/solution.py
@@ -1,3 +1,5 @@
+import functools
+
 import jax
 import jax.numpy as jnp
 from jax import lax
@@ -92,16 +94,21 @@
                 jnp.logical_and(overlaps, line // 2 == b),
             )
 
-    parts = []
-    fill(0)
-    for n in range(len(chunks)):
-        if n + 1 < len(chunks):
-            fill(n + 1)
-        s = score[n][...]
-        top = jnp.max(s, axis=0, keepdims=True)
-        part = top + jnp.log(jnp.sum(jnp.exp(s - top), axis=0, keepdims=True))
-        parts += [part[:, :128], part[:, 128:]]
-    out[...] = jnp.broadcast_to(jnp.concatenate(parts, axis=0)[None], out.shape)
+    def run(t):
+        parts = []
+        fill(4 * t)
+        for n in range(4 * t, 4 * t + 4):
+            if n < 4 * t + 3:
+                fill(n + 1)
+            s = score[n][...]
+            top = jnp.max(s, axis=0, keepdims=True)
+            part = top + jnp.log(jnp.sum(jnp.exp(s - top), axis=0, keepdims=True))
+            parts += [part[:, :128], part[:, 128:]]
+        lines = jnp.concatenate(parts, axis=0)
+        out[:, t * 8 : (t + 1) * 8, :] = jnp.broadcast_to(lines[None], (16, 8, 128))
+
+    for t in range(2):
+        pl.when(core < 2)(functools.partial(run, t))
 
 
 def grad_kernel(own, other, parts, out, score, lse, high, low, picked_rows, students):

time: 83.4 us -> 83.5 us (level)
  no operation moved by 1% of the time
where the time goes in v10:
time: 83.5 us; the launch traced here: 83 us
  blocking collectives  70.7 us (85%)
  Pallas kernels  7 us (8%)
  waiting for transfers between devices  2.63 us (3%)
  starting transfers between devices  1.91 us (2%)
    all_to_all x3, blocking collectives, mixed_exchange(): lax.all_to_all(pieces, AXES, split_axis=0, concat_axis=0, axis_index_grou...  58.5 us
    all_gather x1, blocking collectives, body(): chip = lax.all_gather(mine, 'core', axis=0, tiled=True)  8.37 us
    pallas_call x5, Pallas kernels, call(): pl.pallas_call(kernel, out_shape=jax.ShapeDtypeStruct(shape, dtype), in_s...  7 us
    ppermute x1, waiting for transfers between devices, body(): other = lax.ppermute(own, 'core', [(0, 1), (1, 0)])  2.63 us
    all_gather x1, blocking collectives, body(): parts = lax.all_gather(mixed_exchange(pieces, MIXED), 'core', axis=0)  1.98 us
    ppermute x1, starting transfers between devices, body(): other = lax.ppermute(own, 'core', [(0, 1), (1, 0)])  1.91 us
    all_gather x1, blocking collectives, body(): whole = lax.all_gather(total, 'core', axis=0, tiled=True)  1.9 us
  transfers between devices with their start and end apart: 1, of which 1 were waited for; matrix products, arithmetic and copies ran while one was open for 0% of the time, Pallas kernels for 0%

profile of v10, /device:TPU:1, one launch (start us, length us, event | category | flops | bytes accessed | tf_op | source)
XLA Modules:
  0.0 83.0 jit_solution(10635353306332328875)
XLA Ops:
  0.0 0.7 pad_maximum_fusion
  0.7 8.4 %all_gather.12.mine = bf16[256,128]{1,0:T(8,128)(2,1)S(1)} all-gather(bf16[128,128]{1,0:T(8,128)(2,1)S(1)} %pad_maximum_fusion), channel_id=1, replica_groups=mesh['xh'=2,'z'=8,'y'=8,'xl'=2,'core'=2] {'core'}, dimensions={0}, use_global_device_ids=true | all-gather | bytes 98304 | tf_op jit(solution)/shard_map/all_gather | solution.py:217
  9.1 0.1 shard_map.28
  9.3 24.9 %all_to_all.15.own = bf16[32,64,256]{2,1,0:T(8,128)(2,1)S(1)} all-to-all(bf16[32,64,256]{2,1,0:T(8,128)(2,1)S(1)} %shard_map.28), channel_id=1, replica_groups={{0,2,256,258,4,6,260,262,8,10,264,266,12,14,268,270,16,18,272,274,20,22..., dimensions={0} | all-to-all | bytes 2097152 | tf_op jit(solution)/shard_map/all_to_all | solution.py:38
  34.2 1.9 %collective-permute-start = (bf16[32,64,256]{2,1,0:T(8,128)(2,1)S(1)}, bf16[32,64,256]{2,1,0:T(8,128)(2,1)S(1)}, u32[]{:S(2)}, u32[]{:S(2)}) collective-permute-start(bf16[32,64,256]{2,1,0:T(8,128)(2,1)S(1)} %all_to_all.15.own), channel_id=1, source_target_pairs={{0,1},{1,0},{2,3},{3,2},{4,5},{5,4},{6,7},{7,6},{8,9},{9,8},{10,11... | collective-permute-start | bytes 3145736 | tf_op jit(solution)/shard_map/ppermute | solution.py:220
  36.1 2.6 %collective-permute-done.other = bf16[32,64,256]{2,1,0:T(8,128)(2,1)S(1)} collective-permute-done((bf16[32,64,256]{2,1,0:T(8,128)(2,1)S(1)}, bf16[32,64,256]{2,1,0:T(8,128)(2,1)S(1)}, u32[]{:S(2)}, u32[]{:S(2)}) %collective-permute-start) | collective-permute-done | bytes 1048608 | tf_op jit(solution)/shard_map/ppermute | solution.py:220
  38.7 2.7 %shard_map.29 = f32[16,16,128]{2,1,0:T(8,128)S(1)} custom-call(bf16[32,64,256]{2,1,0:T(8,128)(2,1)S(1)} %all_to_all.15.own, bf16[32,64,256]{2,1,0:T(8,128)(2,1)S(1)} %collective-permute-done.other), custom_call_target="tpu_custom_call" | custom-call | tf_op jit(solution)/shard_map/pallas_call | solution.py:205
  41.5 19.3 %all_to_all.16 = f32[16,16,128]{2,1,0:T(8,128)S(1)} all-to-all(f32[16,16,128]{2,1,0:T(8,128)S(1)} %shard_map.29), channel_id=1, replica_groups={{0,2,4,6,8,10,12,14,16,18,20,22,24,26,28,30},{32,34,36,38,40,42,44,46,4..., dimensions={0} | all-to-all | bytes 262144 | tf_op jit(solution)/shard_map/all_to_all | solution.py:38
  60.8 2.0 %all-gather = f32[32,16,128]{2,1,0:T(8,128)S(1)} all-gather(f32[16,16,128]{2,1,0:T(8,128)S(1)} %all_to_all.16), channel_id=2, replica_groups=mesh['xh'=2,'z'=8,'y'=8,'xl'=2,'core'=2] {'core'}, dimensions={0}, use_global_device_ids=true | all-gather | bytes 393216 | tf_op jit(solution)/shard_map/all_gather | solution.py:224
  62.7 3.3 %shard_map.30 = bf16[32,32,128]{2,1,0:T(8,128)(2,1)S(1)} custom-call(bf16[32,64,256]{2,1,0:T(8,128)(2,1)S(1)} %all_to_all.15.own, bf16[32,64,256]{2,1,0:T(8,128)(2,1)S(1)} %collective-permute-done.other, f32[2,16,16,128]{3,2,1,0:T(8,128)S(1)} %bitcast.4), custom_call_target="tpu_custom_call" | custom-call | tf_op jit(solution)/shard_map/pallas_call | solution.py:205
  66.1 14.3 %all_to_all.17.terms = bf16[32,32,128]{2,1,0:T(8,128)(2,1)S(1)} all-to-all(bf16[32,32,128]{2,1,0:T(8,128)(2,1)S(1)} %shard_map.30), channel_id=1, replica_groups={{0,2,256,258,4,6,260,262,8,10,264,266,12,14,268,270,16,18,272,274,20,22..., dimensions={0} | all-to-all | bytes 524288 | tf_op jit(solution)/shard_map/all_to_all | solution.py:38
  80.4 1.9 %all_gather.15.whole = f32[128,128]{1,0:T(8,128)S(1)} all-gather(f32[64,128]{1,0:T(8,128)S(1)} %shard_map.31), channel_id=1, replica_groups=mesh['xh'=2,'z'=8,'y'=8,'xl'=2,'core'=2] {'core'}, dimensions={0}, use_global_device_ids=true | all-gather | bytes 98304 | tf_op jit(solution)/shard_map/all_gather | solution.py:232
  82.3 0.7 shard_map.32
  (1 shorter events, 0.0 us)
Async XLA Ops:
  34.2 4.5 %collective-permute-start = (bf16[32,64,256]{2,1,0:T(8,128)(2,1)S(1)}, bf16[32,64,256]{2,1,0:T(8,128)(2,1)S(1)}, u32[]{:S(2)}, u32[]{:S(2)}) collective-permute-start(bf16[32,64,256]{2,1,0:T(8,128)(2,1)S(1)} %all_to_all.15.own), channel_id=1, source_target_pairs={{0,1},{1,0},{2,3},{3,2},{4,5},{5,4},{6,7},{7,6},{8,9},{9,8},{10,11... | collective-permute-start | bytes 3145736 | tf_op jit(solution)/shard_map/ppermute | solution.py:220
